TPU v7x, 32 devices: a whole 2x2x4 slice. The times are simulated.
32 devices in a mesh: wide: 8 (over z, x), blk: 4 (over y, core).
Axes of the slice: x: 2, y: 2, z: 4, core: 2. Of those that a mesh axis runs over, the one named last changes fastest.
Arguments:
- tokens: bfloat16 [16, 256, 768], P('wide', 'blk'), may hold values from -21 to 21
- cotangent: bfloat16 [16, 256, 768], P('wide', 'blk'), may hold values from -4 to 4
- row_counts: int32 [16, 4], P('wide', 'blk'), may hold values from 3 to 4, as said below
- mask_flags: int32 [16, 256], P('wide', 'blk'), may hold values from 0 to 1, as said below
- ln1_gain: float32 [768], replicated, may hold values from 0.5 to 1.5
- ln1_bias: float32 [768], replicated, may hold values from -1 to 1
- w_qkv: bfloat16 [768, 2304], replicated, may hold values from -0.21875 to 0.21875
- q_bias: float32 [768], replicated, may hold values from -1 to 1
- v_bias: float32 [768], replicated, may hold values from -1 to 1
- w_out: bfloat16 [768, 768], replicated, may hold values from -1.75 to 1.75
- out_bias: float32 [768], replicated, may hold values from -1 to 1
- ln2_gain: float32 [768], replicated, may hold values from 0.5 to 1.5
- ln2_bias: float32 [768], replicated, may hold values from -1 to 1
- w_fc1: bfloat16 [768, 3072], replicated, may hold values from -0.21875 to 0.21875
- fc1_bias: float32 [3072], replicated, may hold values from -1 to 1
- w_fc2: bfloat16 [3072, 768], replicated, may hold values from -0.109375 to 0.109375
- fc2_bias: float32 [768], replicated, may hold values from -1 to 1
Outputs:
- layer_out: bfloat16 [16, 256, 768], P('wide', 'blk')
- grad_tokens: bfloat16 [16, 256, 768], P('wide', 'blk')
- grad_ln1_gain: float32 [768], replicated
- grad_ln1_bias: float32 [768], replicated
- grad_w_qkv: float32 [768, 2304], replicated
- grad_q_bias: float32 [768], replicated
- grad_v_bias: float32 [768], replicated
- grad_w_out: float32 [768, 768], replicated
- grad_out_bias: float32 [768], replicated
- grad_ln2_gain: float32 [768], replicated
- grad_ln2_bias: float32 [768], replicated
- grad_w_fc1: float32 [768, 3072], replicated
- grad_fc1_bias: float32 [3072], replicated
- grad_w_fc2: float32 [3072, 768], replicated
- grad_fc2_bias: float32 [768], replicated
Inputs may be any that keep to these rules, and one draw needn't show every extreme that they name: `row_counts`: each image's 4 counts are two of 4 and two of 3 in an order drawn for that image; blk index c holds the image's live patches in its first 14 * count slots. `mask_flags`: each image has its own share of ones, between 40 and 80 in 100.
All inputs are finite; a program needn't handle non-finite values.
Results may differ from a plain program's by a relative error of at most 0.015.
Values may be sent and summed in bfloat16 or wider, within the bound.
A program may use at most 192 MiB of HBM per device.

v0:
```python
from functools import partial

import jax
import jax.numpy as jnp
from jax import lax
from jax.sharding import PartitionSpec as P

HEADS = 12
ROW_LEN = 14


EPS = 1e-06


def norm_parts(values_in, norm_gain, norm_bias):
    mean_val = jnp.mean(values_in, -1, keepdims=True)
    centred = values_in - mean_val
    variance = jnp.mean(centred * centred, -1, keepdims=True)
    inverse = lax.rsqrt(variance + EPS)
    unit_val = centred * inverse
    return (unit_val * norm_gain + norm_bias, unit_val, inverse)


def norm_back(grad_in, unit_val, inverse, norm_gain):
    scaled = grad_in * norm_gain
    centred_grad = (
        scaled
        - jnp.mean(scaled, -1, keepdims=True)
        - unit_val * jnp.mean(scaled * unit_val, -1, keepdims=True)
    )
    return (centred_grad * inverse, jnp.sum(grad_in * unit_val, (0, 1)), jnp.sum(grad_in, (0, 1)))


def fold_keys(query_heads, state_in, piece_in, start_at):
    row_top, row_total, accumulated = state_in
    key_piece, value_piece, live_piece = piece_in
    images, key_count = (key_piece.shape[0], key_piece.shape[1])
    head_count, head_width = (query_heads.shape[2], query_heads.shape[3])
    key_heads = key_piece.reshape(images, key_count, head_count, head_width)
    value_heads = value_piece.reshape(images, key_count, head_count, head_width)
    scores = jnp.einsum(
        "iqhe,ikhe->ihqk", query_heads, key_heads, preferred_element_type=jnp.float32
    ) * head_width ** (-0.5)
    key_live = (live_piece > 0.5)[:, None, None, :]
    masked = jnp.where(key_live, scores, -1e30)
    new_top = jnp.maximum(row_top, jnp.max(masked, -1))
    expo_vals = jnp.where(key_live, jnp.exp(masked - new_top[..., None]), 0.0)
    row_total = jnp.sum(expo_vals, -1)
    added = jnp.einsum(
        "ihqk,ikhe->iqhe",
        expo_vals.astype(jnp.bfloat16),
        value_heads,
        preferred_element_type=jnp.float32,
    )
    accumulated = added
    return (new_top, row_total, accumulated)


def pack_grads(tensors, devices, factor):
    flat_vec = jnp.concatenate([tensor.reshape(-1) for tensor in tensors]) * factor
    pad_count = -flat_vec.shape[0] % devices
    return jnp.pad(flat_vec, (0, pad_count))


def unpack_grads(flat_vec, tensors):
    pieces = []
    offset = 0
    for tensor in tensors:
        pieces.append(flat_vec[offset : offset + tensor.size].reshape(tensor.shape))
        offset += tensor.size
    return pieces


def shards(
    tokens,
    cotangent,
    row_counts,
    mask_flags,
    ln1_gain,
    ln1_bias,
    w_qkv,
    q_bias,
    v_bias,
    w_out,
    out_bias,
    ln2_gain,
    ln2_bias,
    w_fc1,
    fc1_bias,
    w_fc2,
    fc2_bias,
):
    images, slot_count, model_width = tokens.shape
    head_count = HEADS
    head_width = model_width // head_count
    score_scale = head_width ** (-0.5)
    limits = row_counts * ROW_LEN
    live_slot = (lax.broadcasted_iota(jnp.int32, (images, slot_count), 1) < limits).astype(
        jnp.float32
    )
    weight = live_slot * mask_flags.astype(jnp.float32)
    start_tok = tokens.astype(jnp.float32)
    normed_first, unit_first, inv_first = norm_parts(start_tok, ln1_gain, ln1_bias)
    normed_first_low = normed_first.astype(jnp.bfloat16)
    qkv_proj = jnp.einsum(
        "isd,de->ise", normed_first_low, w_qkv, preferred_element_type=jnp.float32
    )
    queries = (qkv_proj[..., :model_width] + q_bias).astype(jnp.bfloat16)
    keys_low = qkv_proj[..., model_width : 2 * model_width].astype(jnp.bfloat16)
    values_low = (qkv_proj[..., 2 * model_width :] + v_bias).astype(jnp.bfloat16)
    query_heads = queries.reshape(images, slot_count, head_count, head_width)
    live_low = live_slot.astype(jnp.bfloat16)
    start_state = (
        jnp.full((images, head_count, slot_count), -1e30, jnp.float32),
        jnp.zeros((images, head_count, slot_count), jnp.float32),
        jnp.zeros((images, slot_count, head_count, head_width), jnp.float32),
    )
    fold_fn = partial(fold_keys, query_heads)
    key_all, value_all, live_all = (
        lax.all_gather(keys_low, "blk", axis=1, tiled=True),
        lax.all_gather(values_low, "blk", axis=1, tiled=True),
        lax.all_gather(live_low, "blk", axis=1, tiled=True),
    )
    row_top, row_total, accumulated = fold_fn(start_state, (key_all, value_all, live_all), 0)
    mixed_heads = accumulated / jnp.transpose(row_total, (0, 2, 1))[..., None]
    log_total = row_top + jnp.log(row_total)
    merged = mixed_heads.reshape(images, slot_count, model_width).astype(jnp.bfloat16)
    attn_out = (
        jnp.einsum("isd,de->ise", merged, w_out, preferred_element_type=jnp.float32) + out_bias
    )
    residual = start_tok + attn_out
    normed_second, unit_second, inv_second = norm_parts(residual, ln2_gain, ln2_bias)
    normed_second_low = normed_second.astype(jnp.bfloat16)
    hidden = (
        jnp.einsum("isd,df->isf", normed_second_low, w_fc1, preferred_element_type=jnp.float32)
        + fc1_bias
    )
    activated, gelu_pull = jax.vjp(partial(jax.nn.gelu, approximate=False), hidden)
    activated_low = activated.astype(jnp.bfloat16)
    result = (
        residual
        + jnp.einsum("isf,fd->isd", activated_low, w_fc2, preferred_element_type=jnp.float32)
        + fc2_bias
    )
    layer_out = result.astype(jnp.bfloat16)
    grad_y = cotangent.astype(jnp.float32) * weight[..., None]
    grad_mlp = grad_y.astype(jnp.bfloat16)
    grad_fc2_bias = jnp.sum(grad_y, (0, 1))
    grad_w_fc2 = jnp.einsum(
        "isf,isd->fd", activated_low, grad_mlp, preferred_element_type=jnp.float32
    )
    grad_act = jnp.einsum("isd,fd->isf", grad_mlp, w_fc2, preferred_element_type=jnp.float32)
    grad_hidden = gelu_pull(grad_act)[0].astype(jnp.bfloat16)
    grad_fc1_bias = jnp.sum(grad_hidden, (0, 1), dtype=jnp.float32)
    grad_w_fc1 = jnp.einsum(
        "isd,isf->df", normed_second_low, grad_hidden, preferred_element_type=jnp.float32
    )
    grad_norm_second = jnp.einsum(
        "isf,df->isd", grad_hidden, w_fc1, preferred_element_type=jnp.float32
    )
    grad_resid_norm, grad_ln2_gain, grad_ln2_bias = norm_back(
        grad_norm_second, unit_second, inv_second, ln2_gain
    )
    grad_resid = grad_y + grad_resid_norm
    grad_attn = grad_resid.astype(jnp.bfloat16)
    grad_out_bias = jnp.sum(grad_attn, (0, 1), dtype=jnp.float32)
    grad_w_out = jnp.einsum("isd,ise->de", merged, grad_attn, preferred_element_type=jnp.float32)
    grad_merged = jnp.einsum(
        "ise,de->isd", grad_attn, w_out, preferred_element_type=jnp.float32
    ).astype(jnp.bfloat16)
    devices = lax.axis_size(("wide", "blk"))
    factor = float(images * slot_count * devices) ** (-0.5)
    back_parts = [
        grad_w_out,
        grad_out_bias,
        grad_ln2_gain,
        grad_ln2_bias,
        grad_w_fc1,
        grad_fc1_bias,
        grad_w_fc2,
        grad_fc2_bias,
    ]
    grad_heads = grad_merged.reshape(images, slot_count, head_count, head_width)
    row_delta = jnp.transpose(jnp.sum(grad_heads * mixed_heads, -1), (0, 2, 1))
    key_heads = key_all.reshape(images, -1, head_count, head_width)
    value_heads = value_all.reshape(images, -1, head_count, head_width)
    scores = (
        jnp.einsum("iqhe,ikhe->ihqk", query_heads, key_heads, preferred_element_type=jnp.float32)
        * score_scale
    )
    key_live = (live_all > 0.5)[:, None, None, :]
    probs_f32 = jnp.where(
        key_live, jnp.exp(jnp.where(key_live, scores, -1e30) - log_total[..., None]), 0.0
    )
    probs_low = probs_f32.astype(jnp.bfloat16)
    grad_probs = jnp.einsum(
        "iqhe,ikhe->ihqk", grad_heads, value_heads, preferred_element_type=jnp.float32
    )
    grad_scores = (probs_f32 * (grad_probs - row_delta[..., None])).astype(jnp.bfloat16)
    grad_query = (
        score_scale
        * jnp.einsum("ihqk,ikhe->iqhe", grad_scores, key_heads, preferred_element_type=jnp.float32)
    ).astype(jnp.bfloat16)
    block_count = 1 * lax.axis_size("blk")
    part_scores = grad_scores
    part_probs = probs_low
    part_scores = part_scores.reshape(images, head_count, slot_count, block_count, slot_count)
    part_probs = part_probs.reshape(images, head_count, slot_count, block_count, slot_count)
    term_key = score_scale * jnp.einsum(
        "ihqcj,iqhe->cijhe", part_scores, query_heads, preferred_element_type=jnp.float32
    )
    term_value = jnp.einsum(
        "ihqcj,iqhe->cijhe", part_probs, grad_heads, preferred_element_type=jnp.float32
    )
    term_key = term_key.reshape(block_count, images, slot_count, model_width)
    term_value = term_value.reshape(block_count, images, slot_count, model_width)
    stacked = lax.psum_scatter(
        jnp.concatenate((term_key, term_value), -1).astype(jnp.bfloat16),
        "blk",
        scatter_dimension=0,
        tiled=True,
    ).astype(jnp.float32)
    grad_key = stacked[0, :, :, :model_width].astype(jnp.bfloat16)
    grad_value = stacked[0, :, :, model_width:].astype(jnp.bfloat16)
    grad_query_rows = grad_query.reshape(images, slot_count, model_width)
    grad_qkv = jnp.concatenate((grad_query_rows, grad_key, grad_value), -1)
    grad_q_bias = jnp.sum(grad_query_rows, (0, 1), dtype=jnp.float32)
    grad_v_bias = jnp.sum(grad_value, (0, 1), dtype=jnp.float32)
    grad_w_qkv = jnp.einsum(
        "isd,ise->de", normed_first_low, grad_qkv, preferred_element_type=jnp.float32
    )
    grad_norm_first = jnp.einsum("ise,de->isd", grad_qkv, w_qkv, preferred_element_type=jnp.float32)
    grad_tok_norm, grad_ln1_gain, grad_ln1_bias = norm_back(
        grad_norm_first, unit_first, inv_first, ln1_gain
    )
    grad_tokens = (grad_resid + grad_tok_norm).astype(jnp.bfloat16)
    front_parts = [grad_ln1_gain, grad_ln1_bias, grad_w_qkv, grad_q_bias, grad_v_bias]
    all_parts = front_parts + back_parts
    grads_shard = lax.psum_scatter(
        pack_grads(all_parts, devices, factor), ("wide", "blk"), scatter_dimension=0, tiled=True
    )
    grads_all = lax.all_gather(
        grads_shard.astype(jnp.bfloat16), ("wide", "blk"), axis=0, tiled=True
    ).astype(grads_shard.dtype)
    summed = unpack_grads(grads_all, all_parts)
    return (layer_out, grad_tokens) + tuple(summed)


def solution(mesh):
    placed = (
        P("wide", "blk", None),
        P("wide", "blk", None),
        P("wide", "blk"),
        P("wide", "blk"),
        P(),
        P(),
        P(),
        P(),
        P(),
        P(),
        P(),
        P(),
        P(),
        P(),
        P(),
        P(),
        P(),
    )
    return jax.shard_map(
        shards,
        mesh=mesh,
        in_specs=placed,
        out_specs=(
            P("wide", "blk", None),
            P("wide", "blk", None),
            P(),
            P(),
            P(),
            P(),
            P(),
            P(),
            P(),
            P(),
            P(),
            P(),
            P(),
            P(),
            P(),
        ),
        check_vma=False,
    )
```

profile of v0, /device:TPU:0, one launch (start us, length us, event | category | flops | bytes accessed | tf_op | source)
XLA Modules:
  0.0 1206.0 jit_solution(492887465904164777)
XLA Ops:
  14.9 11.7 all_gather.14
  29.4 5.0 all-gather
  38.6 9.1 all_gather.12
  56.4 3.9 fusion.79
  60.3 4.5 multiply_convert_fusion.2
  80.1 3.5 reshape.169
  87.0 4.4 copy.68
  91.4 3.9 reshape.170
  95.2 3.5 reshape.171
  102.0 4.4 copy.70
  106.4 3.9 reshape.172
  129.2 5.9 copy.79
  135.1 5.2 convolution_bitcast_fusion
  140.3 10.8 reshape.176
  152.2 3.7 fusion.70
  156.0 4.2 convolution_bitcast_fusion.1
  160.2 7.9 reshape.173
  170.7 60.9 %dynamic-update-slice.3 = f32[7087104]{0:T(1024)} dynamic-update-slice(f32[7087104]{0:T(1024)} %constant_dynamic-update-slice_fusion.8, f32[1769472]{0:T(1024)} %reshape.173, s32[]{} %constant.105) | dynamic-update-slice | bytes 14155780
  239.7 80.6 %dynamic-update-slice.10 = f32[7087104]{0:T(1024)} dynamic-update-slice(f32[7087104]{0:T(1024)} %constant_dynamic-update-slice_fusion.2, f32[2359296]{0:T(1024)} %bitcast.105, s32[]{} %constant.112) | dynamic-update-slice | bytes 18874372
  321.6 80.1 %dynamic-update-slice.12 = f32[7087104]{0:T(1024)} dynamic-update-slice(f32[7087104]{0:T(1024)} %constant_dynamic-update-slice_fusion.1, f32[2359296]{0:T(1024)} %reshape.176, s32[]{} %constant.114) | dynamic-update-slice | bytes 18874372
  403.0 20.8 %broadcast_multiply_fusion = f32[7087104]{0:T(1024)} fusion(f32[7087104]{0:T(1024)} %constant_dynamic-update-slice_fusion), kind=kLoop, calls=%fused_computation | loop fusion | flops 7087104 | bytes 56696832 | tf_op jit(solution)/shard_map/mul | solution.py:60
  423.8 459.5 %all-reduce.6 = bf16[7087104]{0:T(1024)(128)(2,1)} all-reduce(f32[7087104]{0:T(1024)} %broadcast_multiply_fusion), channel_id=3, replica_groups=mesh['wide'=8,'blk'=4] {'wide','blk'}, use_global_device_ids=true, to_apply=%region_21.22.clone | all-reduce | flops 7087104 | bytes 42522624
  884.6 5.2 broadcast.118
  889.7 7.5 dynamic-update-slice
  898.6 4.6 fusion.50
  904.1 240.5 %all-reduce.5.cloned.1.call-done = bf16[7087104]{0:T(1024)(128)(2,1)} async-done(((bf16[7087104]{0:T(1024)(128)(2,1)}), bf16[7087104]{0:T(1024)(128)(2,1)}) %all-reduce.5.cloned.1.call-update) | async-done | bytes 14174224
  1144.5 10.0 fusion.92
  1154.6 10.9 reshape.178
  1165.5 11.3 slice.95
  1176.7 4.7 slice.104
  1181.4 8.2 reshape.177
  1192.6 3.4 slice.88
  (193 shorter events, 87.3 us)
Async XLA Ops:
  7.2 143.9 %reduce-scatter.2.cloned.1.call-start = ((), (), s32[]{:S(2)}) async-start(), calls=%async_computation.1 | async-start | bytes 1966080 | tf_op jit(solution)/shard_map/reduce_scatter | solution.py:217
  12.8 16.0 %copy-start.56 = (s32[2,1]{0,1:T(1,128)S(1)}, s32[2,1]{0,1:T(1,128)}, u32[]{:S(2)}) copy-start(s32[2,1]{0,1:T(1,128)} %param.19) | copy-start | bytes 28
  55.8 13.9 %copy-start.4 = (f32[2,64,768]{2,1,0:T(8,128)}, f32[2,64,768]{2,1,0:T(8,128)S(1)}, u32[]{:S(2)}) copy-start(f32[2,64,768]{2,1,0:T(8,128)S(1)} %get-tuple-element.49) | copy-start | bytes 1179652
  56.1 8.8 slice-start
  56.4 13.4 %copy-start.43 = (f32[2,64]{1,0:T(2,128)}, f32[2,64]{1,0:T(2,128)S(1)}, u32[]{:S(2)}) copy-start(f32[2,64]{1,0:T(2,128)S(1)} %convert_select_fusion) | copy-start | bytes 1540
  56.4 8.5 slice-start.1
  56.4 8.5 copy-start.21
  60.3 7.0 slice-start.2
  74.4 4.1 copy-start.3
  74.4 4.1 copy-start.17
  74.4 4.1 copy-start.28
  74.4 4.1 copy-start.36
  112.9 1031.6 %all-reduce.5.cloned.1.call-start = ((), (), s32[]{:S(2)}) async-start(), calls=%async_computation.2 | async-start | bytes 28348416
  129.2 6.0 copy-start.7
  129.2 6.0 copy-start.22
  129.2 5.9 copy-start.44
  140.3 11.8 copy-start.25
  140.3 11.9 copy-start.32
  140.3 11.9 copy-start.34
  160.2 7.9 copy-start.48
  170.7 60.9 %copy-start.41 = (f32[768]{0:T(1024)S(1)}, f32[768]{0:T(1024)}, u32[]{:S(2)}) copy-start(f32[768]{0:T(1024)} %reduce_sum.186) | copy-start | bytes 9220
  170.7 62.2 %copy-start.19 = (bf16[1,2,64,1536]{3,2,1,0:T(8,128)(2,1)S(1)}, bf16[1,2,64,1536]{3,2,1,0:T(8,128)(2,1)}, u32[]{:S(2)}) copy-start(bf16[1,2,64,1536]{3,2,1,0:T(8,128)(2,1)} %reduce-scatter.2.cloned.1.call-done) | copy-start | bytes 1179652
  170.7 63.5 %copy-start.6 = (f32[589824]{0:T(1024)S(1)}, f32[589824]{0:T(1024)}, u32[]{:S(2)}) copy-start(f32[589824]{0:T(1024)} %reshape.174) | copy-start | bytes 7077892
  234.2 4.2 copy-start.38
  239.7 80.6 %copy-start.42 = (f32[3072]{0:T(1024)S(1)}, f32[3072]{0:T(1024)}, u32[]{:S(2)}) copy-start(f32[3072]{0:T(1024)} %get-tuple-element.55) | copy-start | bytes 36868
  321.6 80.1 %copy-start.37 = (f32[768]{0:T(1024)S(1)}, f32[768]{0:T(1024)}, u32[]{:S(2)}) copy-start(f32[768]{0:T(1024)} %get-tuple-element.43) | copy-start | bytes 9220
  898.5 4.6 copy-start.52
  898.6 4.6 copy-start.51
  898.6 4.6 copy-start.11
  898.6 4.6 copy-start.13
  898.6 4.6 copy-start.24
  1189.7 9.0 copy-start.1
  (31 other events, 65.5 us)
Sparse Core Ops, SparseCore 0:
  113.0 28.4 reduce-scatter.1
  897.4 247.0 all-reduce.4
where the time goes:
time: 1230 us; the launch traced here: 1210 us
  blocking collectives  485 us (39%)
  local copies, waits for them, and re-layouts  373 us (30%)
  waiting for transfers between devices  240 us (20%)
  matrix products  51.6 us (4%)
  other arithmetic  40.4 us (3%)
  between operations  15 us (1%)
    unnamed x1, blocking collectives  459 us
    unnamed x138, local copies, waits for them, and re-layouts  257 us
    unnamed x3, waiting for transfers between devices  240 us
    slice x7, local copies, waits for them, and re-layouts, unpack_grads(): pieces.append(flat_vec[offset:offset + tensor.size].reshape(tensor.shape))  35 us
  transfers between devices with their start and end apart: 2, of which 1 were waited for; matrix products, arithmetic and copies ran while one was open for 4% of the time, Pallas kernels for 0%

commit v1 on v0

v1 whole, which is shorter than its diff:
```python
import functools

import jax
import jax.numpy as jnp
from jax import lax
from jax.experimental import pallas as pl
from jax.experimental.pallas import tpu as pltpu
from jax.sharding import PartitionSpec as P

HEADS = 12
ROW_LEN = 14
EPS = 1e-06
RING = 8
BF = jnp.bfloat16
F32 = jnp.float32
MESH = pl.DeviceIdType.MESH
NT = (((1,), (1,)), ((), ()))
TN = (((0,), (0,)), ((), ()))


def dot(a, b, dims=(((1,), (0,)), ((), ()))):
    return lax.dot_general(a, b, dims, preferred_element_type=F32)


def ring_place(r):
    return jnp.where(r % 2 == 0, r // 2, RING - 1 - r // 2)


def ring_member(q):
    return jnp.where(q < RING // 2, 2 * q, 2 * RING - 1 - 2 * q)


def al(v, m):
    return pl.multiple_of(v, m)


class Stream:
    def __init__(self, way, local, final, bufs, kind, rows, cols):
        self.way, self.local, self.final, self.bufs, self.kind = way, local, final, bufs, kind
        self.rows, self.cols = rows, cols


def layer_kernel(n_wide, factor, *refs):
    (
        tok, cot, counts, flags, g1, b1, qb, vb, ob, g2, b2, fb1, fb2, wqkv_h, wout_h, w1_h, w2_h,
        lo_out, gt_out, f2, f1, fq, fo, sall,
        wqkv, wout, w1, w2, xs, cs, meta, n1, n1t, u1, inv1, qkv, probs, mix, mrg, exs, exr, res, n2, n2t, u2, inv2,
        act, gd, gh, gres, ga, gm, gqkv, mps, mpr, lo_s, gt_s, sg, sy, sv,
        l2, l1, lq, lout, r768, r384, rqn, rqp, y768, yqn, yqp, x768, x384, gsh, gsv,
        w_sem, t_send, t_recv, e_send, e_recv, o_send, o_recv,
        rs_send, rs_recv, yb_send, yb_recv, ya_send, ya_recv, ag_send, ag_recv, yg_send, yg_recv,
        c_send, c_recv, s_send, s_recv, g_send, g_recv,
    ) = refs
    groups = n_wide // RING
    seq, width = xs.shape
    half = width // 2
    ffh = w1.shape[1]
    slots = seq // 4
    w = lax.axis_index("wide")
    b = lax.axis_index("blk")
    y, c = b // 2, b % 2
    group, inner = w // RING, w % RING
    p = ring_place(inner)

    def at_place(q):
        return (group * RING + ring_member(lax.rem(q + RING, RING)), b)

    nxt, prv = at_place(p + 1), at_place(p - 1)
    core = (w, 2 * y + 1 - c)
    ydev = (w, 2 * (1 - y) + c)
    ydiag = (w, 2 * (1 - y) + 1 - c)
    others = [(lax.rem(group + j, groups) * RING + inner, b) for j in range(1, groups)]

    bar = pltpu.get_barrier_semaphore()
    greeted = [core, ydev, ydiag, nxt, prv] + others
    for dev in greeted:
        pl.semaphore_signal(bar, inc=1, device_id=dev, device_id_type=MESH)
    half_c = al(c * half, 128)
    ffh_c = al(c * ffh, 128)
    loads = [
        pltpu.make_async_copy(wqkv_h.at[:, pl.ds(al(j * width + c * half, 128), half)], wqkv.at[:, pl.ds(j * half, half)], w_sem.at[j])
        for j in range(3)
    ] + [
        pltpu.make_async_copy(wout_h.at[pl.ds(half_c, half), :], wout, w_sem.at[3]),
        pltpu.make_async_copy(w1_h.at[:, pl.ds(ffh_c, ffh)], w1, w_sem.at[4]),
        pltpu.make_async_copy(w2_h.at[pl.ds(ffh_c, ffh), :], w2, w_sem.at[5]),
    ]
    for load in loads:
        load.start()

    def remote(src, dst, send, recv, dev):
        return pltpu.make_async_remote_copy(
            src_ref=src, dst_ref=dst, send_sem=send, recv_sem=recv, device_id=dev, device_id_type=MESH
        )

    lane64 = lax.broadcasted_iota(jnp.int32, (1, slots), 1)
    zero64 = jnp.zeros((1, slots), F32)
    for img in range(2):
        live = (lane64 < counts[pl.ds(img, 1), :] * ROW_LEN).astype(F32)
        weight = live * flags[pl.ds(img, 1), :].astype(F32)
        for row, val in ((0, live), (1, weight)):
            low = jnp.concatenate([val, zero64], 1)
            high = jnp.concatenate([zero64, val], 1)
            meta[4 + img, pl.ds(row, 1), :] = jnp.where(c == 0, low, high)
    seg = al(b * slots, slots)
    xs[pl.ds(seg, slots), :] = tok[y]
    cs[pl.ds(seg, slots), :] = cot[y]
    meta[b] = meta[4 + y]

    pl.semaphore_wait(bar, len(greeted))
    first = []
    for i, (dev, img) in enumerate(((core, y), (ydev, 1 - y), (ydiag, 1 - y))):
        first.append([
            remote(meta.at[4 + img], meta.at[b], t_send.at[3 * i], t_recv.at[3 * i], dev),
            remote(tok.at[img], xs.at[pl.ds(seg, slots), :], t_send.at[3 * i + 1], t_recv.at[3 * i + 1], dev),
            remote(cot.at[img], cs.at[pl.ds(seg, slots), :], t_send.at[3 * i + 2], t_recv.at[3 * i + 2], dev),
        ])
    for kind in range(3):
        for trio in first:
            trio[kind].start()
    for kind in range(2):
        for trio in first:
            trio[kind].wait_recv()

    blocks = seq // 64

    def rows_of(i):
        return pl.ds(al(i * 64, 64), 64)

    def norm(src, gain, bias, unit_ref, inv_ref, out):
        def body(i, carry):
            r = rows_of(i)
            v = src[r, :].astype(F32)
            cen = v - jnp.mean(v, -1, keepdims=True)
            inv = lax.rsqrt(jnp.mean(cen * cen, -1, keepdims=True) + EPS)
            unit = cen * inv
            unit_ref[r, :] = unit
            inv_ref[r, :] = inv
            out[r, :] = (unit * gain[...] + bias[...]).astype(BF)
            return carry
        lax.fori_loop(0, blocks, body, 0)

    norm(xs, g1, b1, u1, inv1, n1)
    loads[0].wait()
    loads[1].wait()
    loads[2].wait()
    qkv[:, pl.ds(0, half)] = (dot(n1[...], wqkv[:, pl.ds(0, half)]) + qb[:, pl.ds(half_c, half)]).astype(BF)
    qkv[:, pl.ds(half, half)] = dot(n1[...], wqkv[:, pl.ds(half, half)]).astype(BF)
    qkv[:, pl.ds(2 * half, half)] = (
        dot(n1[...], wqkv[:, pl.ds(2 * half, half)]) + vb[:, pl.ds(half_c, half)]
    ).astype(BF)

    live_row = jnp.concatenate([meta[0, 0:1, :] + meta[1, 0:1, :], meta[2, 0:1, :] + meta[3, 0:1, :]], 1)
    weight_row = jnp.concatenate([meta[0, 1:2, :] + meta[1, 1:2, :], meta[2, 1:2, :] + meta[3, 1:2, :]], 1)
    key_live = live_row > 0.5
    lane = lax.broadcasted_iota(jnp.int32, (1, 128), 1)
    low_lanes = lane < 64
    head_mask = [low_lanes.astype(BF), (lane >= 64).astype(BF)]
    head_dim = width // HEADS
    scale = head_dim ** -0.5

    def attend(pair, carry):
        off = al(pair * 128, 128)
        qp = qkv[:, pl.ds(off, 128)]
        kp = qkv[:, pl.ds(al(half + off, 128), 128)]
        vp = qkv[:, pl.ds(al(2 * half + off, 128), 128)]
        outs = []
        for hh in range(2):
            s = dot(qp * head_mask[hh], kp, NT) * scale
            s = jnp.where(key_live, s, -1e30)
            e = jnp.exp(s - jnp.max(s, -1, keepdims=True))
            pr = (e / jnp.sum(e, -1, keepdims=True)).astype(BF)
            probs[2 * pair + hh] = pr
            outs.append(dot(pr, vp))
        o = jnp.where(low_lanes, outs[0], outs[1])
        mix[:, pl.ds(off, 128)] = o
        mrg[:, pl.ds(off, 128)] = o.astype(BF)
        return carry

    lax.fori_loop(0, half // 128, attend, 0)

    def swap(i):
        return remote(exs.at[i], exr.at[i], e_send.at[i], e_recv.at[i], core)

    loads[3].wait()
    exs[0] = dot(mrg[...], wout[...]).astype(BF)
    swap(0).start()
    n1t[...] = n1[...].T
    eye = lax.broadcasted_iota(jnp.int32, (seq, seq), 0) == lax.broadcasted_iota(jnp.int32, (seq, seq), 1)
    weight_col = jnp.sum(jnp.where(eye, weight_row, 0.0), -1, keepdims=True)
    for trio in first:
        trio[2].wait_recv()
    cs[...] = (cs[...].astype(F32) * weight_col).astype(BF)
    swap(0).wait_recv()

    def residual(i, carry):
        r = rows_of(i)
        res[r, :] = xs[r, :].astype(F32) + exs[0, r, :].astype(F32) + exr[0, r, :].astype(F32) + ob[...]
        return carry

    lax.fori_loop(0, blocks, residual, 0)
    norm(res, g2, b2, u2, inv2, n2)
    n2t[...] = n2[...].T
    loads[4].wait()
    tile = 256
    root_half = 0.5 ** 0.5
    pdf_scale = (2.0 * jnp.pi) ** -0.5

    def hidden(j, carry):
        cols = pl.ds(al(j * tile, 128), tile)
        h = dot(n2[...], w1[:, cols]) + fb1[:, pl.ds(al(ffh_c + j * tile, 128), tile)]
        cdf = 0.5 * (1.0 + lax.erf(h * root_half))
        act[:, cols] = (h * cdf).astype(BF)
        gd[:, cols] = cdf + h * (jnp.exp(-0.5 * h * h) * pdf_scale)
        return carry

    lax.fori_loop(0, ffh // tile, hidden, 0)
    loads[5].wait()

    def grad_two(j, carry):
        cols = pl.ds(al(j * tile, 128), tile)
        l2[cols, :] = (dot(act[:, cols], cs[...], TN) * factor).astype(BF)
        d = dot(cs[...], w2[cols, :], NT) * gd[:, cols]
        low = d.astype(BF)
        gh[:, cols] = low
        row = j // 3
        sv[pl.ds(row, 1), pl.ds(al((j - 3 * row) * tile, 128), tile)] = (
            jnp.sum(low.astype(F32), 0, keepdims=True) * factor
        )
        l1[:, cols] = (dot(n2t[...], low) * factor).astype(BF)
        return carry

    lax.fori_loop(0, ffh // tile, grad_two, 0)
    exs[1] = dot(gh[...], w1[...], NT).astype(BF)
    swap(1).start()
    mps[...] = dot(act[...], w2[...]).astype(BF)

    def seg_rows(s):
        return pl.ds(al(s * slots, slots), slots)

    mlp_sends = [
        remote(mps.at[seg_rows(2 * k + 1 - c)], mpr.at[seg_rows(2 * k + 1 - c)], o_send.at[k], o_recv.at[k], core)
        for k in range(2)
    ]
    for send in mlp_sends:
        send.start()
    swap(1).wait_recv()

    zero_row = jnp.zeros((1, width), F32)

    def norm_back(slot, unit_ref, inv_ref, gain, base):
        def body(i, sums):
            r = rows_of(i)
            g = exs[slot, r, :].astype(F32) + exr[slot, r, :].astype(F32)
            unit = unit_ref[r, :]
            scaled = g * gain[...]
            inner_grad = inv_ref[r, :] * (
                scaled - jnp.mean(scaled, -1, keepdims=True) - unit * jnp.mean(scaled * unit, -1, keepdims=True)
            )
            total = base(r) + inner_grad
            gres[r, :] = total
            low = total.astype(BF)
            ga[r, :] = low
            return (
                sums[0] + jnp.sum(g * unit, 0, keepdims=True),
                sums[1] + jnp.sum(g, 0, keepdims=True),
                sums[2] + jnp.sum(low.astype(F32), 0, keepdims=True),
                sums[3] + jnp.sum(cs[r, :].astype(F32), 0, keepdims=True),
            )
        return lax.fori_loop(0, blocks, body, (zero_row,) * 4)

    def mine(row):
        return jnp.where(c == 0, row[:, :half], row[:, half:]) * factor

    s_gain, s_bias, s_out, s_two = norm_back(1, u2, inv2, g2, lambda r: cs[r, :].astype(F32))
    sv[pl.ds(5, 1), pl.ds(0, half)] = mine(s_gain)
    sv[pl.ds(5, 1), pl.ds(half, half)] = mine(s_bias)
    sv[pl.ds(4, 1), pl.ds(0, half)] = mine(s_out)
    sv[pl.ds(4, 1), pl.ds(half, half)] = mine(s_two)
    sv[pl.ds(6, 2), :] = jnp.zeros((2, width), F32)
    lout[...] = (dot(mrg[...], ga[...], TN) * factor).astype(BF)
    gm[...] = dot(ga[...], wout[...], NT).astype(BF)

    def attend_back(pair, carry):
        off = al(pair * 128, 128)
        offk = al(half + off, 128)
        offv = al(2 * half + off, 128)
        qp = qkv[:, pl.ds(off, 128)]
        kp = qkv[:, pl.ds(offk, 128)]
        vp = qkv[:, pl.ds(offv, 128)]
        gmp = gm[:, pl.ds(off, 128)]
        op = mix[:, pl.ds(off, 128)]
        dq, dk, dv = [], [], []
        for hh in range(2):
            gmh = gmp * head_mask[hh]
            gp = dot(gmh, vp, NT)
            delta = jnp.sum(gmh.astype(F32) * op, -1, keepdims=True)
            pr = probs[2 * pair + hh]
            ds = (pr.astype(F32) * (gp - delta)).astype(BF)
            dq.append(dot(ds, kp))
            dk.append(dot(ds, qp, TN))
            dv.append(dot(pr, gmp, TN))
        gqkv[:, pl.ds(off, 128)] = (jnp.where(low_lanes, dq[0], dq[1]) * scale).astype(BF)
        gqkv[:, pl.ds(offk, 128)] = (jnp.where(low_lanes, dk[0], dk[1]) * scale).astype(BF)
        gqkv[:, pl.ds(offv, 128)] = jnp.where(low_lanes, dv[0], dv[1]).astype(BF)
        return carry

    lax.fori_loop(0, half // 128, attend_back, 0)
    for j in range(3):
        cols = pl.ds(j * half, half)
        lq[:, cols] = (dot(n1t[...], gqkv[:, cols]) * factor).astype(BF)
    sv[pl.ds(2, 1), pl.ds(0, half)] = jnp.sum(gqkv[:, pl.ds(0, half)].astype(F32), 0, keepdims=True) * factor
    sv[pl.ds(2, 1), pl.ds(half, half)] = (
        jnp.sum(gqkv[:, pl.ds(2 * half, half)].astype(F32), 0, keepdims=True) * factor
    )
    exs[2] = dot(gqkv[...], wqkv[...], NT).astype(BF)
    swap(2).start()

    def finish(target, landing, value, sends, sem0):
        for k in range(2):
            val = value(seg_rows(2 * k + c)).astype(BF)
            @pl.when(y == k)
            def _():
                target[y] = val
            @pl.when(y != k)
            def _():
                landing[0] = val
        send = remote(landing.at[0], landing.at[1], o_send.at[sem0], o_recv.at[sem0], ydev)
        send.start()
        return send

    for send in mlp_sends:
        send.wait_recv()
    lo_send = finish(
        lo_out, lo_s,
        lambda r: res[r, :] + mps[r, :].astype(F32) + mpr[r, :].astype(F32) + fb2[...], None, 2,
    )
    swap(2).wait_recv()
    s_gain, s_bias, _, _ = norm_back(2, u1, inv1, g1, lambda r: gres[r, :])
    gt_send = finish(gt_out, gt_s, lambda r: gres[r, :], None, 3)
    sv[pl.ds(3, 1), pl.ds(0, half)] = mine(s_gain)
    sv[pl.ds(3, 1), pl.ds(half, half)] = mine(s_bias)

    def chunk(q):
        return lax.rem(q + 2 * RING, RING)

    streams = []
    for way in (1, -1):
        d = 0 if way == 1 else 1
        for sub in range(2):
            i = 2 * d + sub
            streams.append(Stream(
                way,
                functools.partial(lambda k, i: l2.at[pl.ds(al(k * 192 + 48 * i, 16), 48), :], i=i),
                functools.partial(lambda k, i: f2.at[c, pl.ds(al(k * 192 + 48 * i, 16), 48), :], i=i),
                (r768.at[i], x768.at[i], None), "a", 48, width,
            ))
        streams.append(Stream(
            way,
            functools.partial(lambda k, yy, d: l1.at[pl.ds(al(k * 96 + 48 * d, 16), 48), pl.ds(al(yy * width, 128), width)], d=d),
            functools.partial(lambda k, yy, d: f1.at[c, pl.ds(al(k * 96 + 48 * d, 16), 48), pl.ds(al(yy * width, 128), width)], d=d),
            (r768.at[4 + d], None, y768.at[d]), "b", 48, width,
        ))
        lo, n = (0, 640) if d == 0 else (640, 512)
        streams.append(Stream(
            way,
            functools.partial(lambda k, yy, lo, n: lq.at[pl.ds(al(k * 96 + 48 * yy, 16), 48), pl.ds(lo, n)], lo=lo, n=n),
            functools.partial(lambda k, yy, lo, n: fq.at[c, pl.ds(al(k * 96 + 48 * yy, 16), 48), pl.ds(lo, n)], lo=lo, n=n),
            ((rqn, rqp)[d], None, (yqn, yqp)[d]), "b", 48, n,
        ))
        streams.append(Stream(
            way,
            functools.partial(lambda k, d: lout.at[pl.ds(al(k * 48, 16), 48), pl.ds(half * d, half)], d=d),
            functools.partial(lambda k, d: fo.at[c, pl.ds(al(k * 48, 16), 48), pl.ds(half * d, half)], d=d),
            (r384.at[d], x384.at[d], None), "a", 48, half,
        ))
    streams = [s for pair in zip(streams[:5], streams[5:]) for s in pair]
    for i, s in enumerate(streams):
        s.i = i
        s.dev = nxt if s.way == 1 else prv
    a_streams = [s for s in streams if s.kind == "a"]
    b_streams = [s for s in streams if s.kind == "b"]
    for i, s in enumerate(a_streams):
        s.a = i
    for i, s in enumerate(b_streams):
        s.b = i

    def local(s, k):
        return s.local(k) if s.kind == "a" else s.local(k, y)

    def final(s, k, yy=None):
        return s.final(k) if s.kind == "a" else s.final(k, y if yy is None else yy)

    def rs_chunk(s, step):
        return chunk(p - s.way * (1 + step))

    def y_copy(s, step):
        return remote(
            s.local(rs_chunk(s, step), 1 - y), s.bufs[2].at[step], yb_send.at[s.b, step], yb_recv.at[s.b, step], ydev
        )

    for step in range(RING):
        for s in b_streams:
            y_copy(s, step).start()

    s_own = remote(sv, sg.at[p], s_send.at[0], s_recv.at[0], nxt)
    s_own_back = remote(sv, sg.at[p], s_send.at[1], s_recv.at[1], prv)
    s_own.start()
    s_own_back.start()
    sg[p] = sv[...]

    def rs_send_copy(s, step):
        src = local(s, rs_chunk(s, 0)) if (s.kind == "a" and isinstance(step, int) and step == 0) else s.bufs[0].at[step - 1]
        return src

    def rs_copy(s, src, step):
        return remote(src, s.bufs[0].at[step], rs_send.at[s.i], rs_recv.at[s.i, step], s.dev)

    def gathered(s, step):
        total = local(s, rs_chunk(s, step))[...].astype(F32)
        if s.kind == "b":
            y_copy(s, step).wait_recv()
            total = total + s.bufs[2][step].astype(F32)
        return total

    for s in streams:
        if s.kind == "a":
            rs_copy(s, local(s, rs_chunk(s, 0)), 0).start()
        else:
            s.bufs[2][0] = gathered(s, 0).astype(BF)
            rs_copy(s, s.bufs[2].at[0], 0).start()

    def rs_step(step, carry):
        for s in streams:
            total = gathered(s, step)
            rs_copy(s, s.bufs[0].at[step - 1], step - 1).wait()
            s.bufs[0][step - 1] = (total + s.bufs[0][step - 1].astype(F32)).astype(BF)
            rs_copy(s, s.bufs[0].at[step - 1], step).start()
        return carry

    lax.fori_loop(1, RING - 1, rs_step, 0)
    last = RING - 2
    ya = [remote(s.bufs[0].at[last], s.bufs[1], ya_send.at[s.a], ya_recv.at[s.a], ydev) for s in a_streams]
    for s in streams:
        total = gathered(s, RING - 1)
        rs_copy(s, s.bufs[0].at[last], last).wait()
        total = (total + s.bufs[0][last].astype(F32)).astype(BF)
        if s.kind == "a":
            s.bufs[0][last] = total
            ya[s.a].start()
        else:
            final(s, p)[...] = total
    for s in a_streams:
        ya[s.a].wait()
        final(s, p)[...] = (s.bufs[0][last].astype(F32) + s.bufs[1][...].astype(F32)).astype(BF)

    if groups > 1:
        for s in streams:
            slot = gsh.at[s.i, :, :, pl.ds(0, s.cols)]
            slot[group] = final(s, p)[...]
            sends = [
                remote(slot.at[group], slot.at[group], g_send.at[s.i, j], g_recv.at[s.i, j], dev)
                for j, dev in enumerate(others)
            ]
            for send in sends:
                send.start()
            for send in sends:
                send.wait()
            total = slot[0].astype(F32)
            for j in range(1, groups):
                total = total + slot[j].astype(F32)
            final(s, p)[...] = total.astype(BF)

    def ag_chunk(s, step):
        return chunk(p - s.way * step)

    def ag_copy(s, step):
        here = final(s, ag_chunk(s, step))
        return remote(here, here, ag_send.at[s.i], ag_recv.at[s.i, step], s.dev)

    def yg_copy(s, step):
        here = final(s, ag_chunk(s, step))
        return remote(here, here, yg_send.at[s.b, step], yg_recv.at[s.b, step], ydev)

    def core_copy(s, step, yy=None):
        here = final(s, ag_chunk(s, step), yy)
        n = 0 if yy is None else 1
        return remote(here, here, c_send.at[n, s.i, step], c_recv.at[n, s.i, step], core)

    def spread(s, step):
        core_copy(s, step).start()
        if s.kind == "b":
            yg_copy(s, step).start()

    for s in b_streams + a_streams:
        ag_copy(s, 0).start()
        spread(s, 0)

    def y_arrived(s, step):
        yg_copy(s, step).wait_recv()
        core_copy(s, step, 1 - y).start()

    def ag_step(step, carry):
        for s in b_streams + a_streams:
            ag_copy(s, step - 1).wait()
            ag_copy(s, step).start()
            spread(s, step)
            if s.kind == "b":
                y_arrived(s, step - 1)
        return carry

    lax.fori_loop(1, RING - 1, ag_step, 0)
    for s in b_streams + a_streams:
        ag_copy(s, last).wait()
        spread(s, RING - 1)
        if s.kind == "b":
            y_arrived(s, last)
    for s in b_streams:
        y_arrived(s, RING - 1)

    s_own.wait()
    s_own_back.wait()
    for step in range(1, RING // 2):
        onward = remote(sg.at[chunk(p - step)], sg.at[chunk(p - step)], s_send.at[0], s_recv.at[1 + step], nxt)
        onward.start()
        if step < RING // 2 - 1:
            back = remote(sg.at[chunk(p + step)], sg.at[chunk(p + step)], s_send.at[1], s_recv.at[4 + step], prv)
            back.start()
            back.wait()
        onward.wait()
    total = sg[0]
    for k in range(1, RING):
        total = total + sg[k]
    sy[0] = total
    y_small = remote(sy.at[0], sy.at[1], s_send.at[2], s_recv.at[8], ydev)
    y_small.start()
    y_small.wait()
    total = sy[0] + sy[1]
    if groups > 1:
        gsv[group] = total
        sends = [
            remote(gsv.at[group], gsv.at[group], g_send.at[len(streams), j], g_recv.at[len(streams), j], dev)
            for j, dev in enumerate(others)
        ]
        for send in sends:
            send.start()
        for send in sends:
            send.wait()
        total = gsv[0]
        for j in range(1, groups):
            total = total + gsv[j]
    sall[c] = total
    core_small = remote(sall.at[c], sall.at[c], s_send.at[3], s_recv.at[9], core)
    core_small.start()
    core_small.wait()

    lo_send.wait()
    lo_out[1 - y] = lo_s[1]
    gt_send.wait()
    gt_out[1 - y] = gt_s[1]

    for trio in first:
        for copy in trio:
            copy.wait_send()
    for i in range(3):
        swap(i).wait_send()
    for send in mlp_sends:
        send.wait_send()

    def drain(step, carry):
        for s in b_streams:
            y_copy(s, step).wait_send()
            yg_copy(s, step).wait_send()
            core_copy(s, step, 1 - y).wait()
        for s in streams:
            core_copy(s, step).wait()
        return carry

    lax.fori_loop(0, RING, drain, 0)


def write_kernel(f2, f1, fq, fo, sall, o_ln1g, o_ln1b, o_qkv, o_qb, o_vb, o_out, o_ob, o_ln2g, o_ln2b, o_fc1, o_fb1, o_fc2, o_fb2, stage, sems):
    width = f2.shape[2]
    half = width // 2
    ffh = f2.shape[1]
    n_buf = stage.shape[0]
    jobs = []
    for c in range(2):
        for k in range(ffh // 192):
            jobs.append((f2, (c, 192 * k, 192, 0, width), lambda c=c, k=k: o_fc2.at[pl.ds(c * ffh + 192 * k, 192), :]))
        for k in range(width // 192):
            for h in range(2):
                jobs.append((f1, (c, 192 * k, 192, width * h, width), lambda c=c, k=k, h=h: o_fc1.at[pl.ds(192 * k, 192), pl.ds(c * ffh + width * h, width)]))
            for j in range(3):
                jobs.append((fq, (c, 192 * k, 192, half * j, half), lambda c=c, k=k, j=j: o_qkv.at[pl.ds(192 * k, 192), pl.ds(j * width + c * half, half)]))
        for k in range(half // 192):
            jobs.append((fo, (c, 192 * k, 192, 0, width), lambda c=c, k=k: o_out.at[pl.ds(c * half + 192 * k, 192), :]))
    copies = []
    for i, (src, (c, row, rows, col, cols), target) in enumerate(jobs):
        slot = i % n_buf
        if i >= n_buf:
            copies[i - n_buf].wait()
        stage[slot, :, pl.ds(0, cols)] = src[c, pl.ds(row, rows), pl.ds(col, cols)].astype(F32)
        copy = pltpu.make_async_copy(stage.at[slot, :, pl.ds(0, cols)], target(), sems.at[slot])
        copy.start()
        copies.append(copy)
    for c in range(2):
        here = pl.ds(c * half, half)
        o_fb1[:, pl.ds(c * ffh, width)] = sall[c, 0:1, :]
        o_fb1[:, pl.ds(c * ffh + width, width)] = sall[c, 1:2, :]
        for row, lo, hi in ((2, o_qb, o_vb), (3, o_ln1g, o_ln1b), (4, o_ob, o_fb2), (5, o_ln2g, o_ln2b)):
            lo[:, here] = sall[c, row : row + 1, pl.ds(0, half)]
            hi[:, here] = sall[c, row : row + 1, pl.ds(half, half)]
    for copy in copies[-n_buf:]:
        copy.wait()


def shards(n_wide, tokens, cotangent, row_counts, mask_flags, ln1_gain, ln1_bias, w_qkv, q_bias, v_bias, w_out, out_bias, ln2_gain, ln2_bias, w_fc1, fc1_bias, w_fc2, fc2_bias):
    images, slots, width = tokens.shape
    ff = w_fc1.shape[1]
    n_blk = lax.axis_size("blk")
    seq, half, ffh = slots * n_blk, width // 2, ff // 2
    groups = n_wide // RING
    factor = float(images * slots * n_wide * n_blk) ** -0.5
    row = lambda v: v.reshape(1, -1)
    vm, dma = pltpu.VMEM, pltpu.SemaphoreType.DMA
    vspec, anyspec = pl.BlockSpec(memory_space=pltpu.VMEM), pl.BlockSpec(memory_space=pl.ANY)
    n_heads = HEADS // 2
    scratch = [
        vm((width, 3 * half), BF), vm((half, width), BF), vm((width, ffh), BF), vm((ffh, width), BF),
        vm((seq, width), BF), vm((seq, width), BF), vm((6, 8, 128), F32),
        vm((seq, width), BF), vm((width, seq), BF), vm((seq, width), F32), vm((seq, 1), F32),
        vm((seq, 3 * half), BF), vm((n_heads, seq, seq), BF), vm((seq, half), F32), vm((seq, half), BF),
        vm((3, seq, width), BF), vm((3, seq, width), BF), vm((seq, width), F32),
        vm((seq, width), BF), vm((width, seq), BF), vm((seq, width), F32), vm((seq, 1), F32),
        vm((seq, ffh), BF), vm((seq, ffh), F32), vm((seq, ffh), BF), vm((seq, width), F32), vm((seq, width), BF),
        vm((seq, half), BF), vm((seq, 3 * half), BF), vm((seq, width), BF), vm((seq, width), BF),
        vm((2, slots, width), BF), vm((2, slots, width), BF),
        vm((RING, 8, width), F32), vm((2, 8, width), F32), vm((8, width), F32),
        vm((ffh, width), BF), vm((width, ffh), BF), vm((width, 3 * half), BF), vm((half, width), BF),
        vm((6, RING - 1, 48, width), BF), vm((2, RING - 1, 48, half), BF),
        vm((RING - 1, 48, 640), BF), vm((RING - 1, 48, 512), BF),
        vm((2, RING, 48, width), BF), vm((RING, 48, 640), BF), vm((RING, 48, 512), BF),
        vm((4, 48, width), BF), vm((2, 48, half), BF),
        vm((10, groups, 48, width) if groups > 1 else (1, 1, 16, 128), BF),
        vm((groups, 8, width) if groups > 1 else (1, 8, 128), F32),
        dma((6,)), dma((9,)), dma((9,)), dma((3,)), dma((3,)), dma((4,)), dma((4,)),
        dma((10,)), dma((10, RING - 1)), dma((4, RING)), dma((4, RING)), dma((6,)), dma((6,)),
        dma((10,)), dma((10, RING - 1)), dma((4, RING)), dma((4, RING)),
        dma((2, 10, RING)), dma((2, 10, RING)), dma((4,)), dma((10,)),
        dma((11, max(groups - 1, 1))), dma((11, max(groups - 1, 1))),
    ]
    outs = [
        jax.ShapeDtypeStruct(tokens.shape, BF), jax.ShapeDtypeStruct(tokens.shape, BF),
        vm((2, ffh, width), BF), vm((2, width, ffh), BF), vm((2, width, 3 * half), BF), vm((2, half, width), BF),
        vm((2, 8, width), F32),
    ]
    lo, gt, f2, f1, fq, fo, sall = pl.pallas_call(
        functools.partial(layer_kernel, n_wide, factor),
        out_shape=outs,
        in_specs=[vspec] * 13 + [anyspec] * 4,
        out_specs=[vspec] * 7,
        scratch_shapes=scratch,
        compiler_params=pltpu.CompilerParams(collective_id=0, has_side_effects=True, vmem_limit_bytes=46 * 2**20),
        name="layer",
    )(
        tokens, cotangent, row_counts, mask_flags, row(ln1_gain), row(ln1_bias), row(q_bias), row(v_bias), row(out_bias),
        row(ln2_gain), row(ln2_bias), row(fc1_bias), row(fc2_bias), w_qkv, w_out, w_fc1, w_fc2,
    )
    vec = jax.ShapeDtypeStruct((1, width), F32)
    mat = lambda *shape: jax.ShapeDtypeStruct(shape, F32)
    n_buf = 6
    grads = pl.pallas_call(
        write_kernel,
        out_shape=[vec, vec, mat(width, 3 * width), vec, vec, mat(width, width), vec, vec, vec, mat(width, ff), mat(1, ff), mat(ff, width), vec],
        in_specs=[vspec] * 5,
        out_specs=[vspec, vspec, anyspec, vspec, vspec, anyspec, vspec, vspec, vspec, anyspec, vspec, anyspec, vspec],
        scratch_shapes=[vm((n_buf, 192, width), F32), dma((n_buf,))],
        compiler_params=pltpu.CompilerParams(vmem_limit_bytes=8 * 2**20),
        name="write",
    )(f2, f1, fq, fo, sall)
    return (lo, gt) + tuple(g.reshape(-1) if g.shape[0] == 1 else g for g in grads)


def solution(mesh):
    rows, whole = P("wide", "blk", None), P()
    return jax.shard_map(
        functools.partial(shards, mesh.shape["wide"]),
        mesh=mesh,
        in_specs=(rows, rows, P("wide", "blk"), P("wide", "blk")) + (whole,) * 13,
        out_specs=(rows, rows) + (whole,) * 13,
        check_vma=False,
    )
```

time: 1230 us -> 194 us (0.16); the launches traced: 1210 us -> 193 us
  blocking collectives: 485 us -> 0 us
  local copies, waits for them, and re-layouts: 373 us -> 12.8 us
  waiting for transfers between devices: 240 us -> 0 us
  Pallas kernels: 0 us -> 175 us
  matrix products: 51.6 us -> 0 us
  other arithmetic: 40.4 us -> 4.84 us
  between operations: 15 us -> 0.69 us
    unnamed x1 -> x0, blocking collectives: 459 us -> none
    unnamed x138 -> x7, local copies, waits for them, and re-layouts: 257 us -> 2.66 us
    unnamed x3 -> x0, waiting for transfers between devices: 240 us -> none
    pallas_call x0 -> x2, Pallas kernels: none -> 175 us  [the longest x1 165 us: shards(): pl.pallas_call(functools.partial(layer_kernel, n_wide, factor), out_shape...]
    dot_general x18 -> x0, matrix products: 51.6 us -> none  [the longest x1 5.2 us: shards(): jnp.einsum('isf,isd->fd', activated_low, grad_mlp, preferred_element_type...]
    reshape x11 -> x8, local copies, waits for them, and re-layouts: 59.9 us -> 10.1 us  [shards(): row = lambda v: v.reshape(1, -1)]
    slice x8 -> x0, local copies, waits for them, and re-layouts: 35.7 us -> none  [the longest x7 35 us: unpack_grads(): pieces.append(flat_vec[offset:offset + tensor.size].reshape(tensor.shape))]
    all_gather x3 -> x0, blocking collectives: 25.8 us -> none  [the longest x1 11.7 us: shards(): lax.all_gather(keys_low, 'blk', axis=1, tiled=True)]
  transfers between devices with their start and end apart: 2 -> 0, of which waited for: 1 -> 0; matrix products, arithmetic and copies ran while one was open for 4% -> 0% of each run, Pallas kernels for 0% -> 0%
where the time goes in v1:
time: 194 us; the launch traced here: 193 us
  Pallas kernels  175 us (90%)
  local copies, waits for them, and re-layouts  12.8 us (7%)
  other arithmetic  4.84 us (2%)
    pallas_call x1, Pallas kernels, shards(): pl.pallas_call(functools.partial(layer_kernel, n_wide, factor), out_shape...  165 us
    pallas_call x1, Pallas kernels, shards(): pl.pallas_call(write_kernel, out_shape=[vec, vec, mat(width, 3 * width),...  10.3 us
    reshape x8, local copies, waits for them, and re-layouts, shards(): row = lambda v: v.reshape(1, -1)  10.1 us
    pallas_call x8, other arithmetic, shards(): pl.pallas_call(write_kernel, out_shape=[vec, vec, mat(width, 3 * width),...  4.84 us

profile of v1, /device:TPU:0, one launch (start us, length us, event | category | flops | bytes accessed | tf_op | source)
XLA Modules:
  0.0 193.3 jit_solution(16062186198851835724)
XLA Ops:
  0.6 1.3 copy.32.refs_2_
  1.9 1.3 reshape.84.refs_4_
  3.2 1.3 reshape.85.refs_5_
  4.5 1.3 reshape.86.refs_6_
  5.7 1.3 reshape.87.refs_7_
  7.0 1.3 reshape.88.refs_8_
  8.3 1.3 reshape.89.refs_9_
  9.5 1.3 reshape.90.refs_10_
  10.8 1.3 reshape.92.refs_12_
  12.1 164.7 %layer.1 = (bf16[2,64,768]{2,1,0:T(8,128)(2,1)}, bf16[2,64,768]{2,1,0:T(8,128)(2,1)}, bf16[2,1536,768]{2,1,0:T(8,128)(2,1)S(1)}, bf16[2,768,1536]{2,1,0:T(8,128)...) custom-call(bf16[2,64,768]{2,1,0:T(8,128)(2,1)} %refs_0_.1, ...), custom_call_target="tpu_custom_call" | custom-call | tf_op jit(solution)/shard_map/layer/pallas_call | solution.py:658
  176.8 0.0 copy-start.1
  176.8 0.0 copy-start
  176.8 10.3 %write.1 = (f32[1,768]{1,0:T(1,128)S(1)}, f32[1,768]{1,0:T(1,128)S(1)}, f32[768,2304]{1,0:T(8,128)}, f32[1,768]{1,0:T(1,128)S(1)}, f32[1,768]{1,0:T(1,128)S(1)},...) custom-call(bf16[2,1536,768]{2,1,0:T(8,128)(2,1)S(1)} %get-tuple-ele, ...), custom_call_target="tpu_custom_call" | custom-call | tf_op jit(solution)/shard_map/write/pallas_call | solution.py:673
  187.1 0.6 reduce
  187.7 0.6 reduce.1
  188.3 0.6 reduce.2
  188.9 0.6 reduce.3
  189.5 0.6 reduce.4
  190.1 0.6 reduce.5
  190.7 0.6 reduce.6
  191.3 0.6 reduce.7
  191.9 0.0 copy-done.1
  191.9 0.7 copy.35
  192.6 0.0 copy-done
  192.6 0.7 copy.36
Async XLA Ops:
  176.8 15.2 %copy-start.1 = (bf16[2,64,768]{2,1,0:T(8,128)(2,1)S(1)}, bf16[2,64,768]{2,1,0:T(8,128)(2,1)}, u32[]{:S(2)}) copy-start(bf16[2,64,768]{2,1,0:T(8,128)(2,1)} %get-tuple-element.70) | copy-start | bytes 589828
  176.8 15.9 %copy-start = (bf16[2,64,768]{2,1,0:T(8,128)(2,1)S(1)}, bf16[2,64,768]{2,1,0:T(8,128)(2,1)}, u32[]{:S(2)}) copy-start(bf16[2,64,768]{2,1,0:T(8,128)(2,1)} %get-tuple-element.71) | copy-start | bytes 589828

commit v2 on v1

v2 whole, which is shorter than its diff:
```python
import functools

import jax
import jax.numpy as jnp
from jax import lax
from jax.experimental import pallas as pl
from jax.experimental.pallas import tpu as pltpu
from jax.sharding import PartitionSpec as P

HEADS = 12
ROW_LEN = 14
EPS = 1e-06
RING = 8
BF = jnp.bfloat16
F32 = jnp.float32
MESH = pl.DeviceIdType.MESH
NT = (((1,), (1,)), ((), ()))
TN = (((0,), (0,)), ((), ()))


def dot(a, b, dims=(((1,), (0,)), ((), ()))):
    return lax.dot_general(a, b, dims, preferred_element_type=F32)


def ring_place(r):
    return jnp.where(r % 2 == 0, r // 2, RING - 1 - r // 2)


def ring_member(q):
    return jnp.where(q < RING // 2, 2 * q, 2 * RING - 1 - 2 * q)


def al(v, m):
    return pl.multiple_of(v, m)


class Stream:
    def __init__(self, way, dev, kind, start, gather, local, final, bufs, other):
        self.way, self.dev, self.kind, self.start, self.gather = way, dev, kind, start, gather
        self.local, self.final, self.bufs, self.other = local, final, bufs, other


START = {"fc2": 0, "fc1": 2, "out": 3, "qkv": 5}
GATHER = {"fc2": 11, "fc1": 9, "out": 12, "qkv": 12}
SMALL = 8
LOOP = 5
AHEAD = 2


def ORDER(two, one, qkv, out):
    return one + qkv + two + out


def layer_kernel(n_wide, factor, *refs):
    (
        tok, cot, counts, flags, g1_h, b1_h, qb_h, vb_h, ob_h, g2_h, b2_h, fb2_h, fb1_h, wqkv_h, wout_h, w1_h, w2_h,
        lo_out, gt_out, f2, f1, fq, fo, sall,
        wqkv, wout, w1, w2, xs, cs, meta, n1, n1t, u1, inv1, qkv, probs, mix, mrg, exs, exr, res, n2, n2t, u2, inv2,
        act, gd, gh, gres, ga, gm, gqkv, mps, mpr, lo_s, gt_s, sg, sy, sv,
        l2, l1, lq, lout, r96, r48, r384, rqn, rqp, y48, yqn, yqp, x96, x384, gsh, gsv,
        vecs, w_sem, v_sem, t_send, t_recv, e_send, e_recv, o_send, o_recv,
        rs_send, rs_recv, yb_send, yb_recv, ya_send, ya_recv, ag_send, ag_recv, yg_send, yg_recv,
        c_send, c_recv, s_send, s_recv, g_send, g_recv,
    ) = refs
    groups = n_wide // RING
    seq, width = xs.shape
    half = width // 2
    ffh = w1.shape[1]
    slots = seq // 4
    w = lax.axis_index("wide")
    b = lax.axis_index("blk")
    y, c = b // 2, b % 2
    group, inner = w // RING, w % RING
    p = ring_place(inner)

    def at_place(q):
        return (group * RING + ring_member(lax.rem(q + RING, RING)), b)

    nxt, prv = at_place(p + 1), at_place(p - 1)
    core = (w, 2 * y + 1 - c)
    ydev = (w, 2 * (1 - y) + c)
    ydiag = (w, 2 * (1 - y) + 1 - c)
    others = [(lax.rem(group + j, groups) * RING + inner, b) for j in range(1, groups)]

    bar = pltpu.get_barrier_semaphore()
    greeted = [core, ydev, ydiag, nxt, prv] + others
    for dev in greeted:
        pl.semaphore_signal(bar, inc=1, device_id=dev, device_id_type=MESH)
    half_c = al(c * half, 128)
    ffh_c = al(c * ffh, 128)
    loads = [
        pltpu.make_async_copy(wqkv_h.at[:, pl.ds(al(j * width + c * half, 128), half)], wqkv.at[:, pl.ds(j * half, half)], w_sem.at[j])
        for j in range(3)
    ] + [
        pltpu.make_async_copy(wout_h.at[pl.ds(half_c, half), :], wout, w_sem.at[3]),
        pltpu.make_async_copy(w1_h.at[:, pl.ds(ffh_c, ffh)], w1, w_sem.at[4]),
        pltpu.make_async_copy(w2_h.at[pl.ds(ffh_c, ffh), :], w2, w_sem.at[5]),
    ]
    small_loads = [
        pltpu.make_async_copy(vec, vecs.at[i], v_sem.at[i])
        for i, vec in enumerate((g1_h, b1_h, qb_h, vb_h, ob_h, g2_h, b2_h, fb2_h))
    ] + [
        pltpu.make_async_copy(fb1_h.at[pl.ds(i * width, width)], vecs.at[8 + i], v_sem.at[8 + i]) for i in range(2 * ffh // width)
    ]
    g1, b1, qb, vb, ob, g2, b2, fb2 = (vecs.at[pl.ds(i, 1), :] for i in range(8))
    for load in small_loads + loads:
        load.start()

    def remote(src, dst, send, recv, dev):
        return pltpu.make_async_remote_copy(
            src_ref=src, dst_ref=dst, send_sem=send, recv_sem=recv, device_id=dev, device_id_type=MESH
        )

    lane64 = lax.broadcasted_iota(jnp.int32, (1, slots), 1)
    zero64 = jnp.zeros((1, slots), F32)
    for img in range(2):
        live = (lane64 < counts[:, pl.ds(img, 1)] * ROW_LEN).astype(F32)
        weight = live * flags[pl.ds(img, 1), :].astype(F32)
        for row, val in ((0, live), (1, weight)):
            low = jnp.concatenate([val, zero64], 1)
            high = jnp.concatenate([zero64, val], 1)
            meta[4 + img, pl.ds(row, 1), :] = jnp.where(c == 0, low, high)
    seg = al(b * slots, slots)
    xs[pl.ds(seg, slots), :] = tok[y]
    cs[pl.ds(seg, slots), :] = cot[y]
    meta[b] = meta[4 + y]

    pl.semaphore_wait(bar, len(greeted))
    first = []
    for i, (dev, img) in enumerate(((core, y), (ydev, 1 - y), (ydiag, 1 - y))):
        first.append([
            remote(meta.at[4 + img], meta.at[b], t_send.at[3 * i], t_recv.at[3 * i], dev),
            remote(tok.at[img], xs.at[pl.ds(seg, slots), :], t_send.at[3 * i + 1], t_recv.at[3 * i + 1], dev),
            remote(cot.at[img], cs.at[pl.ds(seg, slots), :], t_send.at[3 * i + 2], t_recv.at[3 * i + 2], dev),
        ])
    for kind in range(3):
        for trio in first:
            trio[kind].start()
    for kind in range(2):
        for trio in first:
            trio[kind].wait_recv()

    def chunk(q):
        return lax.rem(q + 2 * RING, RING)

    def streams_of(way):
        d = 0 if way == 1 else 1
        dev = nxt if way == 1 else prv
        lo, n = (0, 640) if d == 0 else (640, 512)
        return [
            Stream(
                way, dev, "a", START["fc2"], GATHER["fc2"],
                lambda k, yy: l2.at[pl.ds(al(k * 192 + 96 * d, 16), 96), :],
                lambda k, yy: f2.at[c, pl.ds(al(k * 192 + 96 * d, 16), 96), :],
                r96.at[d], x96.at[d],
            ),
            Stream(
                way, dev, "b", START["fc1"], GATHER["fc1"],
                lambda k, yy: l1.at[pl.ds(al(k * 96 + 48 * d, 16), 48), pl.ds(al(yy * width, 128), width)],
                lambda k, yy: f1.at[c, pl.ds(al(k * 96 + 48 * d, 16), 48), pl.ds(al(yy * width, 128), width)],
                r48.at[d], y48.at[d],
            ),
            Stream(
                way, dev, "b", START["qkv"], GATHER["qkv"],
                lambda k, yy: lq.at[pl.ds(al(k * 96 + 48 * yy, 16), 48), pl.ds(lo, n)],
                lambda k, yy: fq.at[c, pl.ds(al(k * 96 + 48 * yy, 16), 48), pl.ds(lo, n)],
                (rqn, rqp)[d], (yqn, yqp)[d],
            ),
            Stream(
                way, dev, "a", START["out"], GATHER["out"],
                lambda k, yy: lout.at[pl.ds(al(k * 48, 16), 48), pl.ds(half * d, half)],
                lambda k, yy: fo.at[c, pl.ds(al(k * 48, 16), 48), pl.ds(half * d, half)],
                r384.at[d], x384.at[d],
            ),
        ]

    streams = [s for pair in zip(streams_of(1), streams_of(-1)) for s in pair]
    for kind in "ab":
        for i, s in enumerate(s for s in streams if s.kind == kind):
            s.k = i
    for i, s in enumerate(streams):
        s.i = i
    st2, st1, stq, sto = streams[0:2], streams[2:4], streams[4:6], streams[6:8]
    b_streams = st1 + stq
    last = RING - 2

    def rs_chunk(s, step):
        return chunk(p - s.way * (1 + step))

    def y_copy(s, step):
        return remote(s.local(rs_chunk(s, step), 1 - y), s.other.at[step], yb_send.at[s.k], yb_recv.at[s.k, step], ydev)

    def rs_copy(s, src, step):
        return remote(src, s.bufs.at[step], rs_send.at[s.i], rs_recv.at[s.i, step], s.dev)

    def own(s, step):
        total = s.local(rs_chunk(s, step), y)[...].astype(F32)
        if s.kind == "b":
            y_copy(s, step).wait_recv()
            total = total + s.other[step].astype(F32)
        return total

    def rs_first(s):
        if s.kind == "a":
            rs_copy(s, s.local(rs_chunk(s, 0), y), 0).start()
        else:
            s.other[0] = own(s, 0).astype(BF)
            rs_copy(s, s.other.at[0], 0).start()

    def rs_add(s, step):
        total = own(s, step)
        rs_copy(s, s.bufs.at[step - 1], step - 1).wait()
        s.bufs[step - 1] = (total + s.bufs[step - 1].astype(F32)).astype(BF)

    def rs_step(s, step):
        rs_add(s, step)
        rs_copy(s, s.bufs.at[step - 1], step).start()

    def y_ahead(s, step):
        if s.kind == "b":
            y_copy(s, step).start()

    def ya_copy(s):
        return remote(s.bufs.at[last], s.other, ya_send.at[s.k], ya_recv.at[s.k], ydev)

    def rs_end(s):
        rs_add(s, RING - 1)
        if s.kind == "a":
            ya_copy(s).start()
        else:
            s.final(p, y)[...] = s.bufs[last]

    def over_groups(s):
        piece = s.final(p, y)
        slot = gsh.at[s.i, :, pl.ds(0, piece.shape[0]), pl.ds(0, piece.shape[1])]
        slot[group] = piece[...]
        sends = [
            remote(slot.at[group], slot.at[group], g_send.at[s.i, j], g_recv.at[s.i, j], dev) for j, dev in enumerate(others)
        ]
        for send in sends:
            send.start()
        for send in sends:
            send.wait()
        total = slot[0].astype(F32)
        for j in range(1, groups):
            total = total + slot[j].astype(F32)
        piece[...] = total.astype(BF)

    def ag_chunk(s, step):
        return chunk(p - s.way * step)

    def ag_copy(s, step):
        here = s.final(ag_chunk(s, step), y)
        return remote(here, here, ag_send.at[s.i], ag_recv.at[s.i, step], s.dev)

    def yg_copy(s, step):
        here = s.final(ag_chunk(s, step), y)
        return remote(here, here, yg_send.at[s.k], yg_recv.at[s.k, step], ydev)

    def core_copy(s, step, yy):
        here = s.final(ag_chunk(s, step), yy)
        return remote(here, here, c_send.at[s.i // 2], c_recv.at[s.i // 2], core)

    def spread(s, step):
        core_copy(s, step, y).start()
        if s.kind == "b":
            yg_copy(s, step).start()

    def y_arrived(s, step):
        if s.kind == "b":
            yg_copy(s, step).wait_recv()
            core_copy(s, step, 1 - y).start()

    def ag_first(s):
        if s.kind == "a":
            ya_copy(s).wait()
            s.final(p, y)[...] = (s.bufs[last].astype(F32) + s.other[...].astype(F32)).astype(BF)
        if groups > 1:
            over_groups(s)
        ag_copy(s, 0).start()
        spread(s, 0)

    def ag_step(s, step):
        ag_copy(s, step - 1).wait()
        ag_copy(s, step).start()
        spread(s, step)
        y_arrived(s, step - 1)

    def ag_end(s):
        ag_copy(s, last).wait()
        spread(s, RING - 1)
        y_arrived(s, last)

    def s_copy(k, way):
        at = chunk(p - way * k)
        return remote(sg.at[at], sg.at[at], s_send.at[0 if way == 1 else 1], s_recv.at[k if way == 1 else 4 + k], nxt if way == 1 else prv)

    def s_ring(k):
        if k == 0:
            sg[p] = sv[...]
        if k > 0:
            s_copy(k - 1, 1).wait()
        if 0 < k < RING // 2:
            s_copy(k - 1, -1).wait()
        if k < RING // 2:
            s_copy(k, 1).start()
        if k < RING // 2 - 1:
            s_copy(k, -1).start()

    def s_over_y():
        return remote(sy.at[0], sy.at[1], s_send.at[2], s_recv.at[8], ydev)

    def s_over_core():
        return remote(sall.at[c], sall.at[c], s_send.at[3], s_recv.at[9], core)

    def s_sum():
        s_ring(RING // 2)
        total = sg[0]
        for k in range(1, RING):
            total = total + sg[k]
        sy[0] = total
        s_over_y().start()

    def s_last():
        s_over_y().wait()
        total = sy[0] + sy[1]
        if groups > 1:
            gsv[group] = total
            sends = [
                remote(gsv.at[group], gsv.at[group], g_send.at[len(streams), j], g_recv.at[len(streams), j], dev)
                for j, dev in enumerate(others)
            ]
            for send in sends:
                send.start()
            for send in sends:
                send.wait()
            total = gsv[0]
            for j in range(1, groups):
                total = total + gsv[j]
        sall[c] = total
        s_over_core().start()

    def when(cond, fn):
        if isinstance(cond, bool):
            if cond:
                fn()
        else:
            pl.when(cond)(fn)

    def both(*conds):
        if all(isinstance(v, bool) for v in conds):
            return all(conds)
        return functools.reduce(jnp.logical_and, conds)

    def tick(t):
        for s in ORDER(st2, st1, stq, sto):
            step = t - s.start
            when(step == 0, lambda s=s: rs_first(s))
            when(both(step >= 1, step <= last), lambda s=s, step=step: rs_step(s, step))
            when(step == RING - 1, lambda s=s: rs_end(s))
            if s.kind == "b":
                when(both(step >= 0, step < RING - AHEAD), lambda s=s, step=step: y_ahead(s, step + AHEAD))
            step = t - s.gather
            when(step == 0, lambda s=s: ag_first(s))
            when(both(step >= 1, step <= last), lambda s=s, step=step: ag_step(s, step))
            when(step == RING - 1, lambda s=s: ag_end(s))
            if s.kind == "b":
                when(step == RING, lambda s=s: y_arrived(s, RING - 1))
        if not isinstance(t, int):
            for k in range(RING // 2):
                when(t == SMALL + k, lambda k=k: s_ring(k))
            when(t == SMALL + RING // 2, s_sum)
            when(t == SMALL + RING // 2 + 1, s_last)

    blocks = seq // 64

    def rows_of(i):
        return pl.ds(al(i * 64, 64), 64)

    def norm(src, gain, bias, unit_ref, inv_ref, out):
        def body(i, carry):
            r = rows_of(i)
            v = src[r, :].astype(F32)
            cen = v - jnp.mean(v, -1, keepdims=True)
            inv = lax.rsqrt(jnp.mean(cen * cen, -1, keepdims=True) + EPS)
            unit = cen * inv
            unit_ref[r, :] = unit
            inv_ref[r, :] = inv
            out[r, :] = (unit * gain[...] + bias[...]).astype(BF)
            return carry
        lax.fori_loop(0, blocks, body, 0)

    for load in small_loads:
        load.wait()
    norm(xs, g1, b1, u1, inv1, n1)
    loads[0].wait()
    loads[1].wait()
    loads[2].wait()
    qkv[:, pl.ds(0, half)] = (dot(n1[...], wqkv[:, pl.ds(0, half)]) + qb[:, pl.ds(half_c, half)]).astype(BF)
    qkv[:, pl.ds(half, half)] = dot(n1[...], wqkv[:, pl.ds(half, half)]).astype(BF)
    qkv[:, pl.ds(2 * half, half)] = (
        dot(n1[...], wqkv[:, pl.ds(2 * half, half)]) + vb[:, pl.ds(half_c, half)]
    ).astype(BF)

    live_row = jnp.concatenate([meta[0, 0:1, :] + meta[1, 0:1, :], meta[2, 0:1, :] + meta[3, 0:1, :]], 1)
    weight_row = jnp.concatenate([meta[0, 1:2, :] + meta[1, 1:2, :], meta[2, 1:2, :] + meta[3, 1:2, :]], 1)
    key_live = live_row > 0.5
    lane = lax.broadcasted_iota(jnp.int32, (1, 128), 1)
    low_lanes = lane < 64
    head_mask = [low_lanes.astype(BF), (lane >= 64).astype(BF)]
    head_dim = width // HEADS
    scale = head_dim ** -0.5

    def attend(pair, carry):
        off = al(pair * 128, 128)
        qp = qkv[:, pl.ds(off, 128)]
        kp = qkv[:, pl.ds(al(half + off, 128), 128)]
        vp = qkv[:, pl.ds(al(2 * half + off, 128), 128)]
        outs = []
        for hh in range(2):
            s = dot(qp * head_mask[hh], kp, NT) * scale
            s = jnp.where(key_live, s, -1e30)
            e = jnp.exp(s - jnp.max(s, -1, keepdims=True))
            pr = (e / jnp.sum(e, -1, keepdims=True)).astype(BF)
            probs[2 * pair + hh] = pr
            outs.append(dot(pr, vp))
        o = jnp.where(low_lanes, outs[0], outs[1])
        mix[:, pl.ds(off, 128)] = o
        mrg[:, pl.ds(off, 128)] = o.astype(BF)
        return carry

    lax.fori_loop(0, half // 128, attend, 0)

    def swap(i):
        return remote(exs.at[i], exr.at[i], e_send.at[i], e_recv.at[i], core)

    loads[3].wait()
    exs[0] = dot(mrg[...], wout[...]).astype(BF)
    swap(0).start()
    n1t[...] = n1[...].T
    eye = lax.broadcasted_iota(jnp.int32, (seq, seq), 0) == lax.broadcasted_iota(jnp.int32, (seq, seq), 1)
    weight_col = jnp.sum(jnp.where(eye, weight_row, 0.0), -1, keepdims=True)
    for trio in first:
        trio[2].wait_recv()
    cs[...] = (cs[...].astype(F32) * weight_col).astype(BF)
    swap(0).wait_recv()

    def residual(i, carry):
        r = rows_of(i)
        res[r, :] = xs[r, :].astype(F32) + exs[0, r, :].astype(F32) + exr[0, r, :].astype(F32) + ob[...]
        return carry

    lax.fori_loop(0, blocks, residual, 0)
    norm(res, g2, b2, u2, inv2, n2)
    n2t[...] = n2[...].T
    loads[4].wait()
    tile = 256
    root_half = 0.5 ** 0.5
    pdf_scale = (2.0 * jnp.pi) ** -0.5

    def hidden(j, carry):
        cols = pl.ds(al(j * tile, 128), tile)
        h = dot(n2[...], w1[:, cols]) + vecs[pl.ds(8 + 2 * c + j // 3, 1), pl.ds(al((j - 3 * (j // 3)) * tile, 128), tile)]
        cdf = 0.5 * (1.0 + lax.erf(h * root_half))
        act[:, cols] = (h * cdf).astype(BF)
        gd[:, cols] = cdf + h * (jnp.exp(-0.5 * h * h) * pdf_scale)
        return carry

    lax.fori_loop(0, ffh // tile, hidden, 0)
    loads[5].wait()

    def grad_fc2(j, carry):
        cols = pl.ds(al(j * tile, 128), tile)
        l2[cols, :] = (dot(act[:, cols], cs[...], TN) * factor).astype(BF)
        return carry

    lax.fori_loop(0, ffh // tile, grad_fc2, 0)
    tick(0)

    def grad_hidden(j, carry):
        cols = pl.ds(al(j * tile, 128), tile)
        d = dot(cs[...], w2[cols, :], NT) * gd[:, cols]
        low = d.astype(BF)
        gh[:, cols] = low
        row = j // 3
        sv[pl.ds(row, 1), pl.ds(al((j - 3 * row) * tile, 128), tile)] = (
            jnp.sum(low.astype(F32), 0, keepdims=True) * factor
        )
        return carry

    def grad_fc1(j, carry):
        cols = pl.ds(al(j * tile, 128), tile)
        l1[:, cols] = (dot(n2t[...], gh[:, cols]) * factor).astype(BF)
        return carry

    lax.fori_loop(0, ffh // tile, grad_hidden, 0)
    exs[1] = dot(gh[...], w1[...], NT).astype(BF)
    swap(1).start()
    lax.fori_loop(0, ffh // tile, grad_fc1, 0)
    for step in range(AHEAD):
        for s in st1:
            y_ahead(s, step)
    tick(1)
    mps[...] = dot(act[...], w2[...]).astype(BF)

    def seg_rows(s):
        return pl.ds(al(s * slots, slots), slots)

    mlp_sends = [
        remote(mps.at[seg_rows(2 * k + 1 - c)], mpr.at[seg_rows(2 * k + 1 - c)], o_send.at[k], o_recv.at[k], core)
        for k in range(2)
    ]
    for send in mlp_sends:
        send.start()
    swap(1).wait_recv()

    zero_row = jnp.zeros((1, width), F32)

    def norm_back(slot, unit_ref, inv_ref, gain, base):
        def body(i, sums):
            r = rows_of(i)
            g = exs[slot, r, :].astype(F32) + exr[slot, r, :].astype(F32)
            unit = unit_ref[r, :]
            scaled = g * gain[...]
            inner_grad = inv_ref[r, :] * (
                scaled - jnp.mean(scaled, -1, keepdims=True) - unit * jnp.mean(scaled * unit, -1, keepdims=True)
            )
            total = base(r) + inner_grad
            gres[r, :] = total
            low = total.astype(BF)
            ga[r, :] = low
            return (
                sums[0] + jnp.sum(g * unit, 0, keepdims=True),
                sums[1] + jnp.sum(g, 0, keepdims=True),
                sums[2] + jnp.sum(low.astype(F32), 0, keepdims=True),
                sums[3] + jnp.sum(cs[r, :].astype(F32), 0, keepdims=True),
            )
        return lax.fori_loop(0, blocks, body, (zero_row,) * 4)

    def mine(row):
        return jnp.where(c == 0, row[:, :half], row[:, half:]) * factor

    s_gain, s_bias, s_out, s_two = norm_back(1, u2, inv2, g2, lambda r: cs[r, :].astype(F32))
    sv[pl.ds(5, 1), pl.ds(0, half)] = mine(s_gain)
    sv[pl.ds(5, 1), pl.ds(half, half)] = mine(s_bias)
    sv[pl.ds(4, 1), pl.ds(0, half)] = mine(s_out)
    sv[pl.ds(4, 1), pl.ds(half, half)] = mine(s_two)
    sv[pl.ds(6, 2), :] = jnp.zeros((2, width), F32)
    lout[...] = (dot(mrg[...], ga[...], TN) * factor).astype(BF)
    gm[...] = dot(ga[...], wout[...], NT).astype(BF)
    tick(2)

    def attend_back(pair, carry):
        off = al(pair * 128, 128)
        offk = al(half + off, 128)
        offv = al(2 * half + off, 128)
        qp = qkv[:, pl.ds(off, 128)]
        kp = qkv[:, pl.ds(offk, 128)]
        vp = qkv[:, pl.ds(offv, 128)]
        gmp = gm[:, pl.ds(off, 128)]
        op = mix[:, pl.ds(off, 128)]
        dq, dk, dv = [], [], []
        for hh in range(2):
            gmh = gmp * head_mask[hh]
            gp = dot(gmh, vp, NT)
            delta = jnp.sum(gmh.astype(F32) * op, -1, keepdims=True)
            pr = probs[2 * pair + hh]
            ds = (pr.astype(F32) * (gp - delta)).astype(BF)
            dq.append(dot(ds, kp))
            dk.append(dot(ds, qp, TN))
            dv.append(dot(pr, gmp, TN))
        gqkv[:, pl.ds(off, 128)] = (jnp.where(low_lanes, dq[0], dq[1]) * scale).astype(BF)
        gqkv[:, pl.ds(offk, 128)] = (jnp.where(low_lanes, dk[0], dk[1]) * scale).astype(BF)
        gqkv[:, pl.ds(offv, 128)] = jnp.where(low_lanes, dv[0], dv[1]).astype(BF)
        return carry

    lax.fori_loop(0, half // 128, attend_back, 0)
    tick(3)
    for j in range(3):
        cols = pl.ds(j * half, half)
        lq[:, cols] = (dot(n1t[...], gqkv[:, cols]) * factor).astype(BF)
    sv[pl.ds(2, 1), pl.ds(0, half)] = jnp.sum(gqkv[:, pl.ds(0, half)].astype(F32), 0, keepdims=True) * factor
    sv[pl.ds(2, 1), pl.ds(half, half)] = (
        jnp.sum(gqkv[:, pl.ds(2 * half, half)].astype(F32), 0, keepdims=True) * factor
    )
    for step in range(AHEAD):
        for s in stq:
            y_ahead(s, step)
    exs[2] = dot(gqkv[...], wqkv[...], NT).astype(BF)
    swap(2).start()
    tick(4)

    def finish(target, landing, value, sends, sem0):
        for k in range(2):
            val = value(seg_rows(2 * k + c)).astype(BF)
            @pl.when(y == k)
            def _():
                target[y] = val
            @pl.when(y != k)
            def _():
                landing[0] = val
        send = remote(landing.at[0], landing.at[1], o_send.at[sem0], o_recv.at[sem0], ydev)
        send.start()
        return send

    for send in mlp_sends:
        send.wait_recv()
    lo_send = finish(
        lo_out, lo_s,
        lambda r: res[r, :] + mps[r, :].astype(F32) + mpr[r, :].astype(F32) + fb2[...], None, 2,
    )
    swap(2).wait_recv()
    s_gain, s_bias, _, _ = norm_back(2, u1, inv1, g1, lambda r: gres[r, :])
    gt_send = finish(gt_out, gt_s, lambda r: gres[r, :], None, 3)
    sv[pl.ds(3, 1), pl.ds(0, half)] = mine(s_gain)
    sv[pl.ds(3, 1), pl.ds(half, half)] = mine(s_bias)

    lax.fori_loop(LOOP, max(s.gather + (RING if s.kind == "b" else RING - 1) for s in streams) + 1, lambda t, carry: (tick(t), carry)[1], 0)
    s_over_core().wait()

    lo_send.wait()
    lo_out[1 - y] = lo_s[1]
    gt_send.wait()
    gt_out[1 - y] = gt_s[1]

    for trio in first:
        for copy in trio:
            copy.wait_send()
    for i in range(3):
        swap(i).wait_send()
    for send in mlp_sends:
        send.wait_send()

    for s in b_streams:
        whole = s.other
        remote(whole, whole, yb_send.at[s.k], yb_recv.at[s.k, 0], ydev).wait_send()
        remote(whole, whole, yg_send.at[s.k], yg_recv.at[s.k, 0], ydev).wait_send()
    for i, arr in enumerate((f2, f1, fq, fo)):
        remote(arr.at[c], arr.at[c], c_send.at[i], c_recv.at[i], core).wait()


def write_kernel(
    lo, gt, f2, f1, fq, fo, sall,
    o_lo, o_gt, o_ln1g, o_ln1b, o_qkv, o_qb, o_vb, o_out, o_ob, o_ln2g, o_ln2b, o_fc1, o_fb1, o_fc2, o_fb2,
    stage, sems, small_sems,
):
    width = f2.shape[2]
    half = width // 2
    ffh = f2.shape[1]
    n_buf = stage.shape[0]
    jobs = []
    for c in range(2):
        for k in range(ffh // 192):
            jobs.append((f2, (c, 192 * k, 192, 0, width), lambda c=c, k=k: o_fc2.at[pl.ds(c * ffh + 192 * k, 192), :]))
        for k in range(width // 192):
            for h in range(2):
                jobs.append((f1, (c, 192 * k, 192, width * h, width), lambda c=c, k=k, h=h: o_fc1.at[pl.ds(192 * k, 192), pl.ds(c * ffh + width * h, width)]))
            for j in range(3):
                jobs.append((fq, (c, 192 * k, 192, half * j, half), lambda c=c, k=k, j=j: o_qkv.at[pl.ds(192 * k, 192), pl.ds(j * width + c * half, half)]))
        for k in range(half // 192):
            jobs.append((fo, (c, 192 * k, 192, 0, width), lambda c=c, k=k: o_out.at[pl.ds(c * half + 192 * k, 192), :]))
    small = [(lo, o_lo), (gt, o_gt)]
    for c in range(2):
        for row in range(2):
            small.append((sall.at[c, row], o_fb1.at[pl.ds(c * ffh + row * width, width)]))
        for row, first, second in ((2, o_qb, o_vb), (3, o_ln1g, o_ln1b), (4, o_ob, o_fb2), (5, o_ln2g, o_ln2b)):
            small.append((sall.at[c, row, pl.ds(0, half)], first.at[pl.ds(c * half, half)]))
            small.append((sall.at[c, row, pl.ds(half, half)], second.at[pl.ds(c * half, half)]))
    small = [pltpu.make_async_copy(src, target, small_sems.at[i]) for i, (src, target) in enumerate(small)]
    for copy in small:
        copy.start()
    copies = []
    for i, (src, (c, row, rows, col, cols), target) in enumerate(jobs):
        slot = i % n_buf
        if i >= n_buf:
            copies[i - n_buf].wait()
        stage[slot, :, pl.ds(0, cols)] = src[c, pl.ds(row, rows), pl.ds(col, cols)].astype(F32)
        copy = pltpu.make_async_copy(stage.at[slot, :, pl.ds(0, cols)], target(), sems.at[slot])
        copy.start()
        copies.append(copy)
    for copy in small + copies[-n_buf:]:
        copy.wait()


def shards(n_wide, tokens, cotangent, row_counts, mask_flags, ln1_gain, ln1_bias, w_qkv, q_bias, v_bias, w_out, out_bias, ln2_gain, ln2_bias, w_fc1, fc1_bias, w_fc2, fc2_bias):
    images, slots, width = tokens.shape
    ff = w_fc1.shape[1]
    n_blk = lax.axis_size("blk")
    seq, half, ffh = slots * n_blk, width // 2, ff // 2
    groups = n_wide // RING
    factor = float(images * slots * n_wide * n_blk) ** -0.5
    vm, dma = pltpu.VMEM, pltpu.SemaphoreType.DMA
    vspec, anyspec = pl.BlockSpec(memory_space=pltpu.VMEM), pl.BlockSpec(memory_space=pl.ANY)
    n_heads = HEADS // 2
    scratch = [
        vm((width, 3 * half), BF), vm((half, width), BF), vm((width, ffh), BF), vm((ffh, width), BF),
        vm((seq, width), BF), vm((seq, width), BF), vm((6, 8, 128), F32),
        vm((seq, width), BF), vm((width, seq), BF), vm((seq, width), F32), vm((seq, 1), F32),
        vm((seq, 3 * half), BF), vm((n_heads, seq, seq), BF), vm((seq, half), F32), vm((seq, half), BF),
        vm((3, seq, width), BF), vm((3, seq, width), BF), vm((seq, width), F32),
        vm((seq, width), BF), vm((width, seq), BF), vm((seq, width), F32), vm((seq, 1), F32),
        vm((seq, ffh), BF), vm((seq, ffh), F32), vm((seq, ffh), BF), vm((seq, width), F32), vm((seq, width), BF),
        vm((seq, half), BF), vm((seq, 3 * half), BF), vm((seq, width), BF), vm((seq, width), BF),
        vm((2, slots, width), BF), vm((2, slots, width), BF),
        vm((RING, 8, width), F32), vm((2, 8, width), F32), vm((8, width), F32),
        vm((ffh, width), BF), vm((width, ffh), BF), vm((width, 3 * half), BF), vm((half, width), BF),
        vm((2, RING - 1, 96, width), BF), vm((2, RING - 1, 48, width), BF), vm((2, RING - 1, 48, half), BF),
        vm((RING - 1, 48, 640), BF), vm((RING - 1, 48, 512), BF),
        vm((2, RING, 48, width), BF), vm((RING, 48, 640), BF), vm((RING, 48, 512), BF),
        vm((2, 96, width), BF), vm((2, 48, half), BF),
        vm((8, groups, 96, width) if groups > 1 else (1, 1, 16, 128), BF),
        vm((groups, 8, width) if groups > 1 else (1, 8, 128), F32),
        vm((16, width), F32), dma((6,)), dma((16,)), dma((9,)), dma((9,)), dma((3,)), dma((3,)), dma((4,)), dma((4,)),
        dma((8,)), dma((8, RING - 1)), dma((4,)), dma((4, RING)), dma((4,)), dma((4,)),
        dma((8,)), dma((8, RING - 1)), dma((4,)), dma((4, RING)),
        dma((4,)), dma((4,)), dma((4,)), dma((10,)),
        dma((9, max(groups - 1, 1))), dma((9, max(groups - 1, 1))),
    ]
    outs = [
        vm(tokens.shape, BF), vm(tokens.shape, BF),
        vm((2, ffh, width), BF), vm((2, width, ffh), BF), vm((2, width, 3 * half), BF), vm((2, half, width), BF),
        vm((2, 8, width), F32),
    ]
    lo, gt, f2, f1, fq, fo, sall = pl.pallas_call(
        functools.partial(layer_kernel, n_wide, factor),
        out_shape=outs,
        in_specs=[vspec] * 4 + [anyspec] * 13,
        out_specs=[vspec] * 7,
        scratch_shapes=scratch,
        compiler_params=pltpu.CompilerParams(collective_id=0, has_side_effects=True, vmem_limit_bytes=46 * 2**20),
        name="layer",
    )(
        tokens, cotangent, row_counts.T, mask_flags, ln1_gain, ln1_bias, q_bias, v_bias, out_bias,
        ln2_gain, ln2_bias, fc2_bias, fc1_bias, w_qkv, w_out, w_fc1, w_fc2,
    )
    vec = jax.ShapeDtypeStruct((width,), F32)
    mat = lambda *shape: jax.ShapeDtypeStruct(shape, F32)
    n_buf = 6
    return pl.pallas_call(
        write_kernel,
        out_shape=[
            jax.ShapeDtypeStruct(tokens.shape, BF), jax.ShapeDtypeStruct(tokens.shape, BF),
            vec, vec, mat(width, 3 * width), vec, vec, mat(width, width), vec, vec, vec, mat(width, ff), mat(ff), mat(ff, width), vec,
        ],
        in_specs=[vspec] * 7,
        out_specs=[anyspec] * 15,
        scratch_shapes=[vm((n_buf, 192, width), F32), dma((n_buf,)), dma((24,))],
        compiler_params=pltpu.CompilerParams(vmem_limit_bytes=8 * 2**20),
        name="write",
    )(lo, gt, f2, f1, fq, fo, sall)


def solution(mesh):
    rows, whole = P("wide", "blk", None), P()
    return jax.shard_map(
        functools.partial(shards, mesh.shape["wide"]),
        mesh=mesh,
        in_specs=(rows, rows, P("wide", "blk"), P("wide", "blk")) + (whole,) * 13,
        out_specs=(rows, rows) + (whole,) * 13,
        check_vma=False,
    )
```

time: 194 us -> 153 us (0.79)
  Pallas kernels: 175 us -> 152 us
  local copies, waits for them, and re-layouts: 12.8 us -> 0 us
  other arithmetic: 4.84 us -> 0 us
    pallas_call x1, Pallas kernels: 165 us -> 142 us  [shards(): pl.pallas_call(functools.partial(layer_kernel, n_wide, factor), out_shape...]
    reshape x8 -> x0, local copies, waits for them, and re-layouts: 10.1 us -> none  [shards(): row = lambda v: v.reshape(1, -1)]
    pallas_call x8 -> x0, other arithmetic: 4.84 us -> none  [shards(): pl.pallas_call(write_kernel, out_shape=[vec, vec, mat(width, 3 * width),...]
    unnamed x7 -> x0, local copies, waits for them, and re-layouts: 2.66 us -> none
where the time goes in v2:
time: 153 us
  Pallas kernels  152 us (99%)
    pallas_call x1, Pallas kernels, shards(): pl.pallas_call(functools.partial(layer_kernel, n_wide, factor), out_shape...  142 us
    pallas_call x1, Pallas kernels, shards(): pl.pallas_call(write_kernel, out_shape=[jax.ShapeDtypeStruct(tokens.shape...  10.1 us

profile of v2, /device:TPU:0, one launch (start us, length us, event | category | flops | bytes accessed | tf_op | source)
XLA Modules:
  0.0 152.7 jit_solution(1207499709239011271)
XLA Ops:
  0.7 141.8 %layer.1 = (bf16[2,64,768]{2,1,0:T(8,128)(2,1)S(1)}, bf16[2,64,768]{2,1,0:T(8,128)(2,1)S(1)}, bf16[2,1536,768]{2,1,0:T(8,128)(2,1)S(1)}, bf16[2,768,1536]{2,1,0:...) custom-call(bf16[2,64,768]{2,1,0:T(8,128)(2,1)} %refs_0_.1, ...), custom_call_target="tpu_custom_call" | custom-call | tf_op jit(solution)/shard_map/layer/pallas_call | solution.py:724
  142.5 10.1 %write.1 = (bf16[2,64,768]{2,1,0:T(8,128)(2,1)}, bf16[2,64,768]{2,1,0:T(8,128)(2,1)}, f32[768]{0:T(1024)}, f32[768]{0:T(1024)}, f32[768,2304]{1,0:T(8,128)}, /*i...) custom-call(bf16[2,64,768]{2,1,0:T(8,128)(2,1)S(1)} %get-tuple-eleme, ...), custom_call_target="tpu_custom_call" | custom-call | tf_op jit(solution)/shard_map/write/pallas_call | solution.py:739

commit v3 on v2

--- a/solution.py
+++ b/solution.py
@@ -35,30 +35,33 @@
 
 
 class Stream:
-    def __init__(self, way, dev, kind, start, gather, local, final, bufs, other):
-        self.way, self.dev, self.kind, self.start, self.gather = way, dev, kind, start, gather
-        self.local, self.final, self.bufs, self.other = local, final, bufs, other
-
-
-START = {"fc2": 0, "fc1": 2, "out": 3, "qkv": 5}
-GATHER = {"fc2": 11, "fc1": 9, "out": 12, "qkv": 12}
+    def __init__(self, way, dev, local, final, bufs, other):
+        self.way, self.dev, self.local, self.final = way, dev, local, final
+        self.bufs, self.other = bufs, other
+
+
+class Pair:
+    def __init__(self, i, kind, k, name, array, whole, streams):
+        self.i, self.kind, self.k, self.array, self.whole, self.streams = i, kind, k, array, whole, streams
+        self.start, self.gather = START[name], GATHER[name]
+
+
+START = {"fc2a": 2, "fc2b": 0, "fc1": 2, "out": 4, "qkv": 4}
+GATHER = {"fc2a": 12, "fc2b": 9, "fc1": 11, "out": 12, "qkv": 11}
 SMALL = 8
 LOOP = 5
 AHEAD = 2
-
-
-def ORDER(two, one, qkv, out):
-    return one + qkv + two + out
+ORDER = (2, 1, 0, 3, 4)
 
 
 def layer_kernel(n_wide, factor, *refs):
     (
-        tok, cot, counts, flags, g1_h, b1_h, qb_h, vb_h, ob_h, g2_h, b2_h, fb2_h, fb1_h, wqkv_h, wout_h, w1_h, w2_h,
+        tok, cot, counts_h, flags_h, g1_h, b1_h, qb_h, vb_h, ob_h, g2_h, b2_h, fb2_h, fb1_h, wqkv_h, wout_h, w1_h, w2_h,
         lo_out, gt_out, f2, f1, fq, fo, sall,
         wqkv, wout, w1, w2, xs, cs, meta, n1, n1t, u1, inv1, qkv, probs, mix, mrg, exs, exr, res, n2, n2t, u2, inv2,
         act, gd, gh, gres, ga, gm, gqkv, mps, mpr, lo_s, gt_s, sg, sy, sv,
-        l2, l1, lq, lout, r96, r48, r384, rqn, rqp, y48, yqn, yqp, x96, x384, gsh, gsv,
-        vecs, w_sem, v_sem, t_send, t_recv, e_send, e_recv, o_send, o_recv,
+        l2, l1, lq, lout, r48, r384, rqn, rqp, y48, yqn, yqp, x48, x384, gsh, gsv,
+        vecs, counts, flags, w_sem, v_sem, t_send, t_recv, e_send, e_recv, o_send, o_recv,
         rs_send, rs_recv, yb_send, yb_recv, ya_send, ya_recv, ag_send, ag_recv, yg_send, yg_recv,
         c_send, c_recv, s_send, s_recv, g_send, g_recv,
     ) = refs
@@ -79,15 +82,25 @@
     nxt, prv = at_place(p + 1), at_place(p - 1)
     core = (w, 2 * y + 1 - c)
     ydev = (w, 2 * (1 - y) + c)
-    ydiag = (w, 2 * (1 - y) + 1 - c)
     others = [(lax.rem(group + j, groups) * RING + inner, b) for j in range(1, groups)]
 
     bar = pltpu.get_barrier_semaphore()
-    greeted = [core, ydev, ydiag, nxt, prv] + others
+    greeted = [core, ydev, nxt, prv] + others
     for dev in greeted:
         pl.semaphore_signal(bar, inc=1, device_id=dev, device_id_type=MESH)
     half_c = al(c * half, 128)
     ffh_c = al(c * ffh, 128)
+    seg = al(b * slots, slots)
+    own_rows = [
+        pltpu.make_async_copy(tok.at[y], xs.at[pl.ds(seg, slots), :], v_sem.at[12]),
+        pltpu.make_async_copy(cot.at[y], cs.at[pl.ds(seg, slots), :], v_sem.at[13]),
+    ]
+    marks = [
+        pltpu.make_async_copy(counts_h, counts, v_sem.at[14]),
+        pltpu.make_async_copy(flags_h, flags, v_sem.at[15]),
+    ]
+    for load in marks + own_rows:
+        load.start()
     loads = [
         pltpu.make_async_copy(wqkv_h.at[:, pl.ds(al(j * width + c * half, 128), half)], wqkv.at[:, pl.ds(j * half, half)], w_sem.at[j])
         for j in range(3)
@@ -111,6 +124,22 @@
             src_ref=src, dst_ref=dst, send_sem=send, recv_sem=recv, device_id=dev, device_id_type=MESH
         )
 
+    pl.semaphore_wait(bar, len(greeted))
+    def entry(i, k, img, dev):
+        src = (meta.at[4 + img], tok.at[img], cot.at[img])[k]
+        dst = (meta.at[b], xs.at[pl.ds(seg, slots), :], cs.at[pl.ds(seg, slots), :])[k]
+        return remote(src, dst, t_send.at[3 * i + k], t_recv.at[3 * i + k], dev)
+
+    def onward(k):
+        rows = pl.ds(al((2 * (1 - y) + c) * slots, slots), slots)
+        here = (meta.at[2 * (1 - y) + c], xs.at[rows, :], cs.at[rows, :])[k]
+        return remote(here, here, t_send.at[6 + k], t_recv.at[6 + k], core)
+
+    first = [[entry(0, k, y, core) for k in range(3)], [entry(1, k, 1 - y, ydev) for k in range(3)], [onward(k) for k in range(3)]]
+    for trio in first[:2]:
+        trio[1].start()
+    for load in marks:
+        load.wait()
     lane64 = lax.broadcasted_iota(jnp.int32, (1, slots), 1)
     zero64 = jnp.zeros((1, slots), F32)
     for img in range(2):
@@ -120,122 +149,129 @@
             low = jnp.concatenate([val, zero64], 1)
             high = jnp.concatenate([zero64, val], 1)
             meta[4 + img, pl.ds(row, 1), :] = jnp.where(c == 0, low, high)
-    seg = al(b * slots, slots)
-    xs[pl.ds(seg, slots), :] = tok[y]
-    cs[pl.ds(seg, slots), :] = cot[y]
     meta[b] = meta[4 + y]
-
-    pl.semaphore_wait(bar, len(greeted))
-    first = []
-    for i, (dev, img) in enumerate(((core, y), (ydev, 1 - y), (ydiag, 1 - y))):
-        first.append([
-            remote(meta.at[4 + img], meta.at[b], t_send.at[3 * i], t_recv.at[3 * i], dev),
-            remote(tok.at[img], xs.at[pl.ds(seg, slots), :], t_send.at[3 * i + 1], t_recv.at[3 * i + 1], dev),
-            remote(cot.at[img], cs.at[pl.ds(seg, slots), :], t_send.at[3 * i + 2], t_recv.at[3 * i + 2], dev),
-        ])
-    for kind in range(3):
-        for trio in first:
-            trio[kind].start()
-    for kind in range(2):
-        for trio in first:
-            trio[kind].wait_recv()
+    for k in (0, 2):
+        for trio in first[:2]:
+            trio[k].start()
 
     def chunk(q):
         return lax.rem(q + 2 * RING, RING)
 
-    def streams_of(way):
-        d = 0 if way == 1 else 1
-        dev = nxt if way == 1 else prv
-        lo, n = (0, 640) if d == 0 else (640, 512)
+    def fc2_streams(j):
         return [
             Stream(
-                way, dev, "a", START["fc2"], GATHER["fc2"],
-                lambda k, yy: l2.at[pl.ds(al(k * 192 + 96 * d, 16), 96), :],
-                lambda k, yy: f2.at[c, pl.ds(al(k * 192 + 96 * d, 16), 96), :],
-                r96.at[d], x96.at[d],
-            ),
+                way, dev,
+                lambda k, yy, d=d: l2.at[pl.ds(al(k * 192 + 96 * d + 48 * j, 16), 48), :],
+                lambda k, yy, d=d: f2.at[c, k, pl.ds(96 * d + 48 * j, 48), :],
+                r48.at[2 * j + d], x48.at[2 * j + d],
+            )
+            for d, (way, dev) in enumerate(ways)
+        ]
+
+    ways = ((1, nxt), (-1, prv))
+    core_ways = tuple(
+        (way * (1 - 2 * c), (jnp.where(c == 0, here[0], there[0]), b))
+        for way, here, there in ((1, nxt, prv), (-1, prv, nxt))
+    )
+    split = ((0, 640), (640, 512))
+    pairs = [
+        Pair(0, "a", 0, "fc2a", 0, l2.at[pl.ds(0, 96), :], fc2_streams(0)),
+        Pair(1, "a", 1, "fc2b", 0, l2.at[pl.ds(0, 96), :], fc2_streams(1)),
+        Pair(2, "b", 0, "fc1", 1, l2.at[pl.ds(0, 96), :], [
             Stream(
-                way, dev, "b", START["fc1"], GATHER["fc1"],
-                lambda k, yy: l1.at[pl.ds(al(k * 96 + 48 * d, 16), 48), pl.ds(al(yy * width, 128), width)],
-                lambda k, yy: f1.at[c, pl.ds(al(k * 96 + 48 * d, 16), 48), pl.ds(al(yy * width, 128), width)],
-                r48.at[d], y48.at[d],
-            ),
+                way, dev,
+                lambda k, yy, d=d: l1.at[pl.ds(al(k * 96 + 48 * d, 16), 48), pl.ds(al(yy * width, 128), width)],
+                lambda k, yy, d=d: f1.at[c, k, pl.ds(48 * d, 48), pl.ds(al(yy * width, 128), width)],
+                r48.at[4 + d], y48.at[d],
+            )
+            for d, (way, dev) in enumerate(ways)
+        ]),
+        Pair(3, "b", 1, "qkv", 2, lq.at[pl.ds(0, 48), :], [
             Stream(
-                way, dev, "b", START["qkv"], GATHER["qkv"],
-                lambda k, yy: lq.at[pl.ds(al(k * 96 + 48 * yy, 16), 48), pl.ds(lo, n)],
-                lambda k, yy: fq.at[c, pl.ds(al(k * 96 + 48 * yy, 16), 48), pl.ds(lo, n)],
+                way, dev,
+                lambda k, yy, at=split[d]: lq.at[pl.ds(al(k * 96 + 48 * yy, 16), 48), pl.ds(*at)],
+                lambda k, yy, at=split[d]: fq.at[c, k, pl.ds(al(48 * yy, 16), 48), pl.ds(*at)],
                 (rqn, rqp)[d], (yqn, yqp)[d],
-            ),
+            )
+            for d, (way, dev) in enumerate(core_ways)
+        ]),
+        Pair(4, "a", 2, "out", 3, l2.at[pl.ds(0, 48), :], [
             Stream(
-                way, dev, "a", START["out"], GATHER["out"],
-                lambda k, yy: lout.at[pl.ds(al(k * 48, 16), 48), pl.ds(half * d, half)],
-                lambda k, yy: fo.at[c, pl.ds(al(k * 48, 16), 48), pl.ds(half * d, half)],
+                way, dev,
+                lambda k, yy, d=d: lout.at[pl.ds(al(k * 48, 16), 48), pl.ds(half * d, half)],
+                lambda k, yy, d=d: fo.at[c, k, :, pl.ds(half * d, half)],
                 r384.at[d], x384.at[d],
-            ),
-        ]
-
-    streams = [s for pair in zip(streams_of(1), streams_of(-1)) for s in pair]
-    for kind in "ab":
-        for i, s in enumerate(s for s in streams if s.kind == kind):
-            s.k = i
-    for i, s in enumerate(streams):
-        s.i = i
-    st2, st1, stq, sto = streams[0:2], streams[2:4], streams[4:6], streams[6:8]
-    b_streams = st1 + stq
+            )
+            for d, (way, dev) in enumerate(ways)
+        ]),
+    ]
+    fc1_pair, qkv_pair = pairs[2], pairs[3]
+    b_pairs = [fc1_pair, qkv_pair]
     last = RING - 2
 
     def rs_chunk(s, step):
         return chunk(p - s.way * (1 + step))
 
-    def y_copy(s, step):
-        return remote(s.local(rs_chunk(s, step), 1 - y), s.other.at[step], yb_send.at[s.k], yb_recv.at[s.k, step], ydev)
-
-    def rs_copy(s, src, step):
-        return remote(src, s.bufs.at[step], rs_send.at[s.i], rs_recv.at[s.i, step], s.dev)
-
-    def own(s, step):
+    def arrived(a, sem):
+        remote(a.whole, a.whole, sem, sem, core).wait_recv()
+
+    def left(a, sem):
+        remote(a.whole, a.whole, sem, sem, core).wait_send()
+
+    def y_ahead(a, step):
+        for s in a.streams:
+            remote(
+                s.local(rs_chunk(s, step), 1 - y), s.other.at[step], yb_send.at[a.k], yb_recv.at[a.k, step], ydev
+            ).start()
+
+    def own(a, s, step):
         total = s.local(rs_chunk(s, step), y)[...].astype(F32)
-        if s.kind == "b":
-            y_copy(s, step).wait_recv()
+        if a.kind == "b":
             total = total + s.other[step].astype(F32)
         return total
 
-    def rs_first(s):
-        if s.kind == "a":
-            rs_copy(s, s.local(rs_chunk(s, 0), y), 0).start()
-        else:
-            s.other[0] = own(s, 0).astype(BF)
-            rs_copy(s, s.other.at[0], 0).start()
-
-    def rs_add(s, step):
-        total = own(s, step)
-        rs_copy(s, s.bufs.at[step - 1], step - 1).wait()
-        s.bufs[step - 1] = (total + s.bufs[step - 1].astype(F32)).astype(BF)
-
-    def rs_step(s, step):
-        rs_add(s, step)
-        rs_copy(s, s.bufs.at[step - 1], step).start()
-
-    def y_ahead(s, step):
-        if s.kind == "b":
-            y_copy(s, step).start()
-
-    def ya_copy(s):
-        return remote(s.bufs.at[last], s.other, ya_send.at[s.k], ya_recv.at[s.k], ydev)
-
-    def rs_end(s):
-        rs_add(s, RING - 1)
-        if s.kind == "a":
-            ya_copy(s).start()
-        else:
-            s.final(p, y)[...] = s.bufs[last]
-
-    def over_groups(s):
+    def rs_send_on(a, s, src, step):
+        remote(src, s.bufs.at[step], rs_send.at[a.i], rs_recv.at[a.i, step], s.dev).start()
+
+    def rs_first(a):
+        if a.kind == "b":
+            arrived(a, yb_recv.at[a.k, 0])
+        for s in a.streams:
+            if a.kind == "a":
+                rs_send_on(a, s, s.local(rs_chunk(s, 0), y), 0)
+            else:
+                s.other[0] = own(a, s, 0).astype(BF)
+                rs_send_on(a, s, s.other.at[0], 0)
+
+    def rs_arrived(a, step):
+        if a.kind == "b":
+            arrived(a, yb_recv.at[a.k, step])
+        arrived(a, rs_recv.at[a.i, step - 1])
+        left(a, rs_send.at[a.i])
+
+    def rs_step(a, step):
+        rs_arrived(a, step)
+        for s in a.streams:
+            s.bufs[step - 1] = (own(a, s, step) + s.bufs[step - 1].astype(F32)).astype(BF)
+            rs_send_on(a, s, s.bufs.at[step - 1], step)
+
+    def rs_end(a):
+        rs_arrived(a, RING - 1)
+        for s in a.streams:
+            total = (own(a, s, RING - 1) + s.bufs[last].astype(F32)).astype(BF)
+            if a.kind == "a":
+                s.bufs[last] = total
+                remote(s.bufs.at[last], s.other, ya_send.at[a.k], ya_recv.at[a.k], ydev).start()
+            else:
+                s.final(p, y)[...] = total
+
+    def over_groups(a, d):
+        s, i = a.streams[d], 2 * a.i + d
         piece = s.final(p, y)
-        slot = gsh.at[s.i, :, pl.ds(0, piece.shape[0]), pl.ds(0, piece.shape[1])]
+        slot = gsh.at[i, :, pl.ds(0, piece.shape[0]), pl.ds(0, piece.shape[1])]
         slot[group] = piece[...]
         sends = [
-            remote(slot.at[group], slot.at[group], g_send.at[s.i, j], g_recv.at[s.i, j], dev) for j, dev in enumerate(others)
+            remote(slot.at[group], slot.at[group], g_send.at[i, j], g_recv.at[i, j], dev) for j, dev in enumerate(others)
         ]
         for send in sends:
             send.start()
@@ -246,50 +282,51 @@
             total = total + slot[j].astype(F32)
         piece[...] = total.astype(BF)
 
-    def ag_chunk(s, step):
-        return chunk(p - s.way * step)
-
-    def ag_copy(s, step):
-        here = s.final(ag_chunk(s, step), y)
-        return remote(here, here, ag_send.at[s.i], ag_recv.at[s.i, step], s.dev)
-
-    def yg_copy(s, step):
-        here = s.final(ag_chunk(s, step), y)
-        return remote(here, here, yg_send.at[s.k], yg_recv.at[s.k, step], ydev)
-
-    def core_copy(s, step, yy):
-        here = s.final(ag_chunk(s, step), yy)
-        return remote(here, here, c_send.at[s.i // 2], c_recv.at[s.i // 2], core)
-
-    def spread(s, step):
-        core_copy(s, step, y).start()
-        if s.kind == "b":
-            yg_copy(s, step).start()
-
-    def y_arrived(s, step):
-        if s.kind == "b":
-            yg_copy(s, step).wait_recv()
-            core_copy(s, step, 1 - y).start()
-
-    def ag_first(s):
-        if s.kind == "a":
-            ya_copy(s).wait()
-            s.final(p, y)[...] = (s.bufs[last].astype(F32) + s.other[...].astype(F32)).astype(BF)
+    def ag_send_on(a, step):
+        for s in a.streams:
+            here = s.final(chunk(p - s.way * step), y)
+            remote(here, here, ag_send.at[a.i], ag_recv.at[a.i, step], s.dev).start()
+
+    def spread(a, step):
+        for s in a.streams:
+            here = s.final(chunk(p - s.way * step), y)
+            if a.kind == "b":
+                remote(here, here, yg_send.at[a.k], yg_recv.at[a.k, step], ydev).start()
+            remote(here, here, c_send.at[a.array], c_recv.at[a.array], core).start()
+
+    def y_arrived(a, step):
+        if a.kind == "b":
+            arrived(a, yg_recv.at[a.k, step])
+            for s in a.streams:
+                here = s.final(chunk(p - s.way * step), 1 - y)
+                remote(here, here, c_send.at[a.array], c_recv.at[a.array], core).start()
+
+    def ag_first(a):
+        if a.kind == "a":
+            arrived(a, ya_recv.at[a.k])
+            left(a, ya_send.at[a.k])
+            for s in a.streams:
+                s.final(p, y)[...] = (s.bufs[last].astype(F32) + s.other[...].astype(F32)).astype(BF)
         if groups > 1:
-            over_groups(s)
-        ag_copy(s, 0).start()
-        spread(s, 0)
-
-    def ag_step(s, step):
-        ag_copy(s, step - 1).wait()
-        ag_copy(s, step).start()
-        spread(s, step)
-        y_arrived(s, step - 1)
-
-    def ag_end(s):
-        ag_copy(s, last).wait()
-        spread(s, RING - 1)
-        y_arrived(s, last)
+            for d in range(2):
+                over_groups(a, d)
+        ag_send_on(a, 0)
+        spread(a, 0)
+
+    def ag_step(a, step):
+        arrived(a, ag_recv.at[a.i, step - 1])
+        left(a, ag_send.at[a.i])
+        ag_send_on(a, step)
+        spread(a, step)
+        y_arrived(a, step - 1)
+
+    def ag_end(a):
+        arrived(a, ag_recv.at[a.i, last])
+        left(a, ag_send.at[a.i])
+        spread(a, RING - 1)
+        y_arrived(a, last)
+
+    y_bytes = [f1.at[c, :, pl.ds(0, 48), :], fq.at[c, :, pl.ds(0, 48), :]]
 
     def s_copy(k, way):
         at = chunk(p - way * k)
@@ -327,7 +364,7 @@
         if groups > 1:
             gsv[group] = total
             sends = [
-                remote(gsv.at[group], gsv.at[group], g_send.at[len(streams), j], g_recv.at[len(streams), j], dev)
+                remote(gsv.at[group], gsv.at[group], g_send.at[10, j], g_recv.at[10, j], dev)
                 for j, dev in enumerate(others)
             ]
             for send in sends:
@@ -353,19 +390,20 @@
         return functools.reduce(jnp.logical_and, conds)
 
     def tick(t):
-        for s in ORDER(st2, st1, stq, sto):
-            step = t - s.start
-            when(step == 0, lambda s=s: rs_first(s))
-            when(both(step >= 1, step <= last), lambda s=s, step=step: rs_step(s, step))
-            when(step == RING - 1, lambda s=s: rs_end(s))
-            if s.kind == "b":
-                when(both(step >= 0, step < RING - AHEAD), lambda s=s, step=step: y_ahead(s, step + AHEAD))
-            step = t - s.gather
-            when(step == 0, lambda s=s: ag_first(s))
-            when(both(step >= 1, step <= last), lambda s=s, step=step: ag_step(s, step))
-            when(step == RING - 1, lambda s=s: ag_end(s))
-            if s.kind == "b":
-                when(step == RING, lambda s=s: y_arrived(s, RING - 1))
+        for i in ORDER:
+            a = pairs[i]
+            step = t - a.start
+            when(step == 0, lambda a=a: rs_first(a))
+            when(both(step >= 1, step <= last), lambda a=a, step=step: rs_step(a, step))
+            when(step == RING - 1, lambda a=a: rs_end(a))
+            if a.kind == "b":
+                when(both(step >= 0, step < RING - AHEAD), lambda a=a, step=step: y_ahead(a, step + AHEAD))
+            step = t - a.gather
+            when(step == 0, lambda a=a: ag_first(a))
+            when(both(step >= 1, step <= last), lambda a=a, step=step: ag_step(a, step))
+            when(step == RING - 1, lambda a=a: ag_end(a))
+            if a.kind == "b":
+                when(step == RING, lambda a=a: y_arrived(a, RING - 1))
         if not isinstance(t, int):
             for k in range(RING // 2):
                 when(t == SMALL + k, lambda k=k: s_ring(k))
@@ -377,9 +415,9 @@
     def rows_of(i):
         return pl.ds(al(i * 64, 64), 64)
 
-    def norm(src, gain, bias, unit_ref, inv_ref, out):
+    def norm(src, gain, bias, unit_ref, inv_ref, out, start=0, count=blocks):
         def body(i, carry):
-            r = rows_of(i)
+            r = rows_of(start + i)
             v = src[r, :].astype(F32)
             cen = v - jnp.mean(v, -1, keepdims=True)
             inv = lax.rsqrt(jnp.mean(cen * cen, -1, keepdims=True) + EPS)
@@ -388,23 +426,37 @@
             inv_ref[r, :] = inv
             out[r, :] = (unit * gain[...] + bias[...]).astype(BF)
             return carry
-        lax.fori_loop(0, blocks, body, 0)
-
-    for load in small_loads:
+        lax.fori_loop(0, count, body, 0)
+
+    def project(yy):
+        norm(xs, g1, b1, u1, inv1, n1, 2 * yy, 2)
+        r = pl.ds(al(yy * 2 * slots, 2 * slots), 2 * slots)
+        rows = n1[r, :]
+        qkv[r, pl.ds(0, half)] = (dot(rows, wqkv[:, pl.ds(0, half)]) + qb[:, pl.ds(half_c, half)]).astype(BF)
+        qkv[r, pl.ds(half, half)] = dot(rows, wqkv[:, pl.ds(half, half)]).astype(BF)
+        qkv[r, pl.ds(2 * half, half)] = (
+            dot(rows, wqkv[:, pl.ds(2 * half, half)]) + vb[:, pl.ds(half_c, half)]
+        ).astype(BF)
+
+    for load in small_loads + loads[:3]:
         load.wait()
-    norm(xs, g1, b1, u1, inv1, n1)
-    loads[0].wait()
-    loads[1].wait()
-    loads[2].wait()
-    qkv[:, pl.ds(0, half)] = (dot(n1[...], wqkv[:, pl.ds(0, half)]) + qb[:, pl.ds(half_c, half)]).astype(BF)
-    qkv[:, pl.ds(half, half)] = dot(n1[...], wqkv[:, pl.ds(half, half)]).astype(BF)
-    qkv[:, pl.ds(2 * half, half)] = (
-        dot(n1[...], wqkv[:, pl.ds(2 * half, half)]) + vb[:, pl.ds(half_c, half)]
-    ).astype(BF)
+    own_rows[0].wait()
+    first[0][1].wait_recv()
+    project(y)
+    first[1][1].wait_recv()
+    first[2][1].start()
+    first[1][0].wait_recv()
+    first[2][0].start()
+    first[2][1].wait_recv()
+    project(1 - y)
+    first[1][2].wait_recv()
+    first[2][2].start()
+    first[0][0].wait_recv()
+    first[2][0].wait_recv()
 
     live_row = jnp.concatenate([meta[0, 0:1, :] + meta[1, 0:1, :], meta[2, 0:1, :] + meta[3, 0:1, :]], 1)
     weight_row = jnp.concatenate([meta[0, 1:2, :] + meta[1, 1:2, :], meta[2, 1:2, :] + meta[3, 1:2, :]], 1)
-    key_live = live_row > 0.5
+    dead = jnp.where(live_row > 0.5, 0.0, -1e30)
     lane = lax.broadcasted_iota(jnp.int32, (1, 128), 1)
     low_lanes = lane < 64
     head_mask = [low_lanes.astype(BF), (lane >= 64).astype(BF)]
@@ -419,9 +471,9 @@
         outs = []
         for hh in range(2):
             s = dot(qp * head_mask[hh], kp, NT) * scale
-            s = jnp.where(key_live, s, -1e30)
+            s = s + dead
             e = jnp.exp(s - jnp.max(s, -1, keepdims=True))
-            pr = (e / jnp.sum(e, -1, keepdims=True)).astype(BF)
+            pr = (e * (1.0 / jnp.sum(e, -1, keepdims=True))).astype(BF)
             probs[2 * pair + hh] = pr
             outs.append(dot(pr, vp))
         o = jnp.where(low_lanes, outs[0], outs[1])
@@ -440,8 +492,9 @@
     n1t[...] = n1[...].T
     eye = lax.broadcasted_iota(jnp.int32, (seq, seq), 0) == lax.broadcasted_iota(jnp.int32, (seq, seq), 1)
     weight_col = jnp.sum(jnp.where(eye, weight_row, 0.0), -1, keepdims=True)
-    for trio in first:
-        trio[2].wait_recv()
+    own_rows[1].wait()
+    first[0][2].wait_recv()
+    first[2][2].wait()
     cs[...] = (cs[...].astype(F32) * weight_col).astype(BF)
     swap(0).wait_recv()
 
@@ -498,8 +551,7 @@
     swap(1).start()
     lax.fori_loop(0, ffh // tile, grad_fc1, 0)
     for step in range(AHEAD):
-        for s in st1:
-            y_ahead(s, step)
+        y_ahead(fc1_pair, step)
     tick(1)
     mps[...] = dot(act[...], w2[...]).astype(BF)
 
@@ -584,8 +636,7 @@
         jnp.sum(gqkv[:, pl.ds(2 * half, half)].astype(F32), 0, keepdims=True) * factor
     )
     for step in range(AHEAD):
-        for s in stq:
-            y_ahead(s, step)
+        y_ahead(qkv_pair, step)
     exs[2] = dot(gqkv[...], wqkv[...], NT).astype(BF)
     swap(2).start()
     tick(4)
@@ -615,7 +666,7 @@
     sv[pl.ds(3, 1), pl.ds(0, half)] = mine(s_gain)
     sv[pl.ds(3, 1), pl.ds(half, half)] = mine(s_bias)
 
-    lax.fori_loop(LOOP, max(s.gather + (RING if s.kind == "b" else RING - 1) for s in streams) + 1, lambda t, carry: (tick(t), carry)[1], 0)
+    lax.fori_loop(LOOP, max(a.gather + (RING if a.kind == "b" else RING - 1) for a in pairs) + 1, lambda t, carry: (tick(t), carry)[1], 0)
     s_over_core().wait()
 
     lo_send.wait()
@@ -623,18 +674,16 @@
     gt_send.wait()
     gt_out[1 - y] = gt_s[1]
 
-    for trio in first:
-        for copy in trio:
-            copy.wait_send()
+    for copy in first[0] + first[1] + first[2][:2]:
+        copy.wait_send()
     for i in range(3):
         swap(i).wait_send()
     for send in mlp_sends:
         send.wait_send()
 
-    for s in b_streams:
-        whole = s.other
-        remote(whole, whole, yb_send.at[s.k], yb_recv.at[s.k, 0], ydev).wait_send()
-        remote(whole, whole, yg_send.at[s.k], yg_recv.at[s.k, 0], ydev).wait_send()
+    for a in b_pairs:
+        remote(y_bytes[a.k], y_bytes[a.k], yb_send.at[a.k], yb_recv.at[a.k, 0], ydev).wait_send()
+        remote(y_bytes[a.k], y_bytes[a.k], yg_send.at[a.k], yg_recv.at[a.k, 0], ydev).wait_send()
     for i, arr in enumerate((f2, f1, fq, fo)):
         remote(arr.at[c], arr.at[c], c_send.at[i], c_recv.at[i], core).wait()
 
@@ -644,21 +693,21 @@
     o_lo, o_gt, o_ln1g, o_ln1b, o_qkv, o_qb, o_vb, o_out, o_ob, o_ln2g, o_ln2b, o_fc1, o_fb1, o_fc2, o_fb2,
     stage, sems, small_sems,
 ):
-    width = f2.shape[2]
+    width = f2.shape[3]
     half = width // 2
-    ffh = f2.shape[1]
+    ffh = f2.shape[1] * f2.shape[2]
     n_buf = stage.shape[0]
     jobs = []
     for c in range(2):
-        for k in range(ffh // 192):
-            jobs.append((f2, (c, 192 * k, 192, 0, width), lambda c=c, k=k: o_fc2.at[pl.ds(c * ffh + 192 * k, 192), :]))
-        for k in range(width // 192):
+        for k in range(RING):
+            jobs.append((f2, c, [k], 0, width, o_fc2.at[pl.ds(c * ffh + 192 * k, 192), :]))
+        for k in range(0, RING, 2):
             for h in range(2):
-                jobs.append((f1, (c, 192 * k, 192, width * h, width), lambda c=c, k=k, h=h: o_fc1.at[pl.ds(192 * k, 192), pl.ds(c * ffh + width * h, width)]))
+                jobs.append((f1, c, [k, k + 1], width * h, width, o_fc1.at[pl.ds(96 * k, 192), pl.ds(c * ffh + width * h, width)]))
             for j in range(3):
-                jobs.append((fq, (c, 192 * k, 192, half * j, half), lambda c=c, k=k, j=j: o_qkv.at[pl.ds(192 * k, 192), pl.ds(j * width + c * half, half)]))
-        for k in range(half // 192):
-            jobs.append((fo, (c, 192 * k, 192, 0, width), lambda c=c, k=k: o_out.at[pl.ds(c * half + 192 * k, 192), :]))
+                jobs.append((fq, c, [k, k + 1], half * j, half, o_qkv.at[pl.ds(96 * k, 192), pl.ds(j * width + c * half, half)]))
+        for k in range(0, RING, 4):
+            jobs.append((fo, c, [k, k + 1, k + 2, k + 3], 0, width, o_out.at[pl.ds(c * half + 48 * k, 192), :]))
     small = [(lo, o_lo), (gt, o_gt)]
     for c in range(2):
         for row in range(2):
@@ -670,12 +719,14 @@
     for copy in small:
         copy.start()
     copies = []
-    for i, (src, (c, row, rows, col, cols), target) in enumerate(jobs):
+    for i, (src, c, chunks, col, cols, target) in enumerate(jobs):
         slot = i % n_buf
         if i >= n_buf:
             copies[i - n_buf].wait()
-        stage[slot, :, pl.ds(0, cols)] = src[c, pl.ds(row, rows), pl.ds(col, cols)].astype(F32)
-        copy = pltpu.make_async_copy(stage.at[slot, :, pl.ds(0, cols)], target(), sems.at[slot])
+        rows = 192 // len(chunks)
+        for at, k in enumerate(chunks):
+            stage[slot, pl.ds(at * rows, rows), pl.ds(0, cols)] = src[c, k, :, pl.ds(col, cols)].astype(F32)
+        copy = pltpu.make_async_copy(stage.at[slot, :, pl.ds(0, cols)], target, sems.at[slot])
         copy.start()
         copies.append(copy)
     for copy in small + copies[-n_buf:]:
@@ -704,27 +755,28 @@
         vm((2, slots, width), BF), vm((2, slots, width), BF),
         vm((RING, 8, width), F32), vm((2, 8, width), F32), vm((8, width), F32),
         vm((ffh, width), BF), vm((width, ffh), BF), vm((width, 3 * half), BF), vm((half, width), BF),
-        vm((2, RING - 1, 96, width), BF), vm((2, RING - 1, 48, width), BF), vm((2, RING - 1, 48, half), BF),
+        vm((6, RING - 1, 48, width), BF), vm((2, RING - 1, 48, half), BF),
         vm((RING - 1, 48, 640), BF), vm((RING - 1, 48, 512), BF),
         vm((2, RING, 48, width), BF), vm((RING, 48, 640), BF), vm((RING, 48, 512), BF),
-        vm((2, 96, width), BF), vm((2, 48, half), BF),
-        vm((8, groups, 96, width) if groups > 1 else (1, 1, 16, 128), BF),
+        vm((4, 48, width), BF), vm((2, 48, half), BF),
+        vm((10, groups, 48, width) if groups > 1 else (1, 1, 16, 128), BF),
         vm((groups, 8, width) if groups > 1 else (1, 8, 128), F32),
-        vm((16, width), F32), dma((6,)), dma((16,)), dma((9,)), dma((9,)), dma((3,)), dma((3,)), dma((4,)), dma((4,)),
-        dma((8,)), dma((8, RING - 1)), dma((4,)), dma((4, RING)), dma((4,)), dma((4,)),
-        dma((8,)), dma((8, RING - 1)), dma((4,)), dma((4, RING)),
+        vm((16, width), F32), vm((1, 2), jnp.int32), vm((2, slots), jnp.int32), dma((6,)), dma((16,)), dma((9,)), dma((9,)), dma((3,)), dma((3,)), dma((4,)), dma((4,)),
+        dma((5,)), dma((5, RING - 1)), dma((2,)), dma((2, RING)), dma((3,)), dma((3,)),
+        dma((5,)), dma((5, RING - 1)), dma((2,)), dma((2, RING)),
         dma((4,)), dma((4,)), dma((4,)), dma((10,)),
-        dma((9, max(groups - 1, 1))), dma((9, max(groups - 1, 1))),
+        dma((11 if groups > 1 else 1, max(groups - 1, 1))), dma((11 if groups > 1 else 1, max(groups - 1, 1))),
     ]
     outs = [
         vm(tokens.shape, BF), vm(tokens.shape, BF),
-        vm((2, ffh, width), BF), vm((2, width, ffh), BF), vm((2, width, 3 * half), BF), vm((2, half, width), BF),
+        vm((2, RING, ffh // RING, width), BF), vm((2, RING, width // RING, ffh), BF),
+        vm((2, RING, width // RING, 3 * half), BF), vm((2, RING, half // RING, width), BF),
         vm((2, 8, width), F32),
     ]
     lo, gt, f2, f1, fq, fo, sall = pl.pallas_call(
         functools.partial(layer_kernel, n_wide, factor),
         out_shape=outs,
-        in_specs=[vspec] * 4 + [anyspec] * 13,
+        in_specs=[anyspec] * 17,
         out_specs=[vspec] * 7,
         scratch_shapes=scratch,
         compiler_params=pltpu.CompilerParams(collective_id=0, has_side_effects=True, vmem_limit_bytes=46 * 2**20),

time: 153 us -> 142 us (0.928)
  Pallas kernels: 152 us -> 141 us
    pallas_call x1, Pallas kernels: 142 us -> 131 us  [shards(): pl.pallas_call(functools.partial(layer_kernel, n_wide, factor), out_shape...]
where the time goes in v3:
time: 142 us
  Pallas kernels  141 us (99%)
    pallas_call x1, Pallas kernels, shards(): pl.pallas_call(functools.partial(layer_kernel, n_wide, factor), out_shape...  131 us
    pallas_call x1, Pallas kernels, shards(): pl.pallas_call(write_kernel, out_shape=[jax.ShapeDtypeStruct(tokens.shape...  10.1 us

profile of v3, /device:TPU:0, one launch (start us, length us, event | category | flops | bytes accessed | tf_op | source)
XLA Modules:
  0.0 141.7 jit_solution(8807603703910088415)
XLA Ops:
  0.7 130.9 %layer.1 = (bf16[2,64,768]{2,1,0:T(8,128)(2,1)S(1)}, bf16[2,64,768]{2,1,0:T(8,128)(2,1)S(1)}, bf16[2,8,192,768]{3,2,1,0:T(8,128)(2,1)S(1)}, bf16[2,8,96,1536]{3,...) custom-call(bf16[2,64,768]{2,1,0:T(8,128)(2,1)} %refs_0_.1, ...), custom_call_target="tpu_custom_call" | custom-call | tf_op jit(solution)/shard_map/layer/pallas_call | solution.py:776
  131.5 10.1 %write.1 = (bf16[2,64,768]{2,1,0:T(8,128)(2,1)}, bf16[2,64,768]{2,1,0:T(8,128)(2,1)}, f32[768]{0:T(1024)}, f32[768]{0:T(1024)}, f32[768,2304]{1,0:T(8,128)}, /*i...) custom-call(bf16[2,64,768]{2,1,0:T(8,128)(2,1)S(1)} %get-tuple-eleme, ...), custom_call_target="tpu_custom_call" | custom-call | tf_op jit(solution)/shard_map/write/pallas_call | solution.py:791

commit v4 on v3

--- a/solution.py
+++ b/solution.py
@@ -46,12 +46,12 @@
         self.start, self.gather = START[name], GATHER[name]
 
 
-START = {"fc2a": 2, "fc2b": 0, "fc1": 2, "out": 4, "qkv": 4}
-GATHER = {"fc2a": 12, "fc2b": 9, "fc1": 11, "out": 12, "qkv": 11}
+START = {"fc2a": 1, "fc2b": 0, "fc1": 2, "out": 5, "qkv": 5}
+GATHER = {"fc2a": 12, "fc2b": 9, "fc1": 11, "out": 13, "qkv": 12}
 SMALL = 8
 LOOP = 5
 AHEAD = 2
-ORDER = (2, 1, 0, 3, 4)
+ORDER = (1, 4, 3, 2, 0)
 
 
 def layer_kernel(n_wide, factor, *refs):
@@ -426,7 +426,7 @@
             inv_ref[r, :] = inv
             out[r, :] = (unit * gain[...] + bias[...]).astype(BF)
             return carry
-        lax.fori_loop(0, count, body, 0)
+        lax.fori_loop(0, count, body, 0, unroll=2)
 
     def project(yy):
         norm(xs, g1, b1, u1, inv1, n1, 2 * yy, 2)
@@ -481,7 +481,7 @@
         mrg[:, pl.ds(off, 128)] = o.astype(BF)
         return carry
 
-    lax.fori_loop(0, half // 128, attend, 0)
+    lax.fori_loop(0, half // 128, attend, 0, unroll=3)
 
     def swap(i):
         return remote(exs.at[i], exr.at[i], e_send.at[i], e_recv.at[i], core)
@@ -503,7 +503,7 @@
         res[r, :] = xs[r, :].astype(F32) + exs[0, r, :].astype(F32) + exr[0, r, :].astype(F32) + ob[...]
         return carry
 
-    lax.fori_loop(0, blocks, residual, 0)
+    lax.fori_loop(0, blocks, residual, 0, unroll=2)
     norm(res, g2, b2, u2, inv2, n2)
     n2t[...] = n2[...].T
     loads[4].wait()
@@ -519,7 +519,7 @@
         gd[:, cols] = cdf + h * (jnp.exp(-0.5 * h * h) * pdf_scale)
         return carry
 
-    lax.fori_loop(0, ffh // tile, hidden, 0)
+    lax.fori_loop(0, ffh // tile, hidden, 0, unroll=3)
     loads[5].wait()
 
     def grad_fc2(j, carry):
@@ -527,7 +527,7 @@
         l2[cols, :] = (dot(act[:, cols], cs[...], TN) * factor).astype(BF)
         return carry
 
-    lax.fori_loop(0, ffh // tile, grad_fc2, 0)
+    lax.fori_loop(0, ffh // tile, grad_fc2, 0, unroll=3)
     tick(0)
 
     def grad_hidden(j, carry):
@@ -546,10 +546,10 @@
         l1[:, cols] = (dot(n2t[...], gh[:, cols]) * factor).astype(BF)
         return carry
 
-    lax.fori_loop(0, ffh // tile, grad_hidden, 0)
+    lax.fori_loop(0, ffh // tile, grad_hidden, 0, unroll=3)
     exs[1] = dot(gh[...], w1[...], NT).astype(BF)
     swap(1).start()
-    lax.fori_loop(0, ffh // tile, grad_fc1, 0)
+    lax.fori_loop(0, ffh // tile, grad_fc1, 0, unroll=3)
     for step in range(AHEAD):
         y_ahead(fc1_pair, step)
     tick(1)
@@ -587,7 +587,7 @@
                 sums[2] + jnp.sum(low.astype(F32), 0, keepdims=True),
                 sums[3] + jnp.sum(cs[r, :].astype(F32), 0, keepdims=True),
             )
-        return lax.fori_loop(0, blocks, body, (zero_row,) * 4)
+        return lax.fori_loop(0, blocks, body, (zero_row,) * 4, unroll=2)
 
     def mine(row):
         return jnp.where(c == 0, row[:, :half], row[:, half:]) * factor
@@ -626,7 +626,7 @@
         gqkv[:, pl.ds(offv, 128)] = jnp.where(low_lanes, dv[0], dv[1]).astype(BF)
         return carry
 
-    lax.fori_loop(0, half // 128, attend_back, 0)
+    lax.fori_loop(0, half // 128, attend_back, 0, unroll=3)
     tick(3)
     for j in range(3):
         cols = pl.ds(j * half, half)

time: 142 us -> 136 us (0.958)
  Pallas kernels: 141 us -> 135 us
    pallas_call x1, Pallas kernels: 131 us -> 125 us  [shards(): pl.pallas_call(functools.partial(layer_kernel, n_wide, factor), out_shape...]
where the time goes in v4:
time: 136 us
  Pallas kernels  135 us (99%)
    pallas_call x1, Pallas kernels, shards(): pl.pallas_call(functools.partial(layer_kernel, n_wide, factor), out_shape...  125 us
    pallas_call x1, Pallas kernels, shards(): pl.pallas_call(write_kernel, out_shape=[jax.ShapeDtypeStruct(tokens.shape...  10.1 us

profile of v4, /device:TPU:0, one launch (start us, length us, event | category | flops | bytes accessed | tf_op | source)
XLA Modules:
  0.0 136.0 jit_solution(10678861310172030153)
XLA Ops:
  0.7 125.1 %layer.1 = (bf16[2,64,768]{2,1,0:T(8,128)(2,1)S(1)}, bf16[2,64,768]{2,1,0:T(8,128)(2,1)S(1)}, bf16[2,8,192,768]{3,2,1,0:T(8,128)(2,1)S(1)}, bf16[2,8,96,1536]{3,...) custom-call(bf16[2,64,768]{2,1,0:T(8,128)(2,1)} %refs_0_.1, ...), custom_call_target="tpu_custom_call" | custom-call | tf_op jit(solution)/shard_map/layer/pallas_call | solution.py:776
  125.8 10.1 %write.1 = (bf16[2,64,768]{2,1,0:T(8,128)(2,1)}, bf16[2,64,768]{2,1,0:T(8,128)(2,1)}, f32[768]{0:T(1024)}, f32[768]{0:T(1024)}, f32[768,2304]{1,0:T(8,128)}, /*i...) custom-call(bf16[2,64,768]{2,1,0:T(8,128)(2,1)S(1)} %get-tuple-eleme, ...), custom_call_target="tpu_custom_call" | custom-call | tf_op jit(solution)/shard_map/write/pallas_call | solution.py:791

commit v5 on v4

--- a/solution.py
+++ b/solution.py
@@ -487,8 +487,14 @@
         return remote(exs.at[i], exr.at[i], e_send.at[i], e_recv.at[i], core)
 
     loads[3].wait()
-    exs[0] = dot(mrg[...], wout[...]).astype(BF)
-    swap(0).start()
+    def swap_rows(k):
+        r = pl.ds(k * (seq // 2), seq // 2)
+        return remote(exs.at[0, r, :], exr.at[0, r, :], e_send.at[3 * k], e_recv.at[3 * k], core)
+
+    for k in range(2):
+        r = pl.ds(k * (seq // 2), seq // 2)
+        exs[0, r, :] = dot(mrg[r, :], wout[...]).astype(BF)
+        swap_rows(k).start()
     n1t[...] = n1[...].T
     eye = lax.broadcasted_iota(jnp.int32, (seq, seq), 0) == lax.broadcasted_iota(jnp.int32, (seq, seq), 1)
     weight_col = jnp.sum(jnp.where(eye, weight_row, 0.0), -1, keepdims=True)
@@ -496,15 +502,16 @@
     first[0][2].wait_recv()
     first[2][2].wait()
     cs[...] = (cs[...].astype(F32) * weight_col).astype(BF)
-    swap(0).wait_recv()
 
     def residual(i, carry):
         r = rows_of(i)
         res[r, :] = xs[r, :].astype(F32) + exs[0, r, :].astype(F32) + exr[0, r, :].astype(F32) + ob[...]
         return carry
 
-    lax.fori_loop(0, blocks, residual, 0, unroll=2)
-    norm(res, g2, b2, u2, inv2, n2)
+    for k in range(2):
+        swap_rows(k).wait_recv()
+        lax.fori_loop(2 * k, 2 * k + 2, residual, 0, unroll=2)
+        norm(res, g2, b2, u2, inv2, n2, 2 * k, 2)
     n2t[...] = n2[...].T
     loads[4].wait()
     tile = 256
@@ -676,8 +683,8 @@
 
     for copy in first[0] + first[1] + first[2][:2]:
         copy.wait_send()
-    for i in range(3):
-        swap(i).wait_send()
+    for copy in (swap_rows(0), swap_rows(1), swap(1), swap(2)):
+        copy.wait_send()
     for send in mlp_sends:
         send.wait_send()
 
@@ -761,7 +768,7 @@
         vm((4, 48, width), BF), vm((2, 48, half), BF),
         vm((10, groups, 48, width) if groups > 1 else (1, 1, 16, 128), BF),
         vm((groups, 8, width) if groups > 1 else (1, 8, 128), F32),
-        vm((16, width), F32), vm((1, 2), jnp.int32), vm((2, slots), jnp.int32), dma((6,)), dma((16,)), dma((9,)), dma((9,)), dma((3,)), dma((3,)), dma((4,)), dma((4,)),
+        vm((16, width), F32), vm((1, 2), jnp.int32), vm((2, slots), jnp.int32), dma((6,)), dma((16,)), dma((9,)), dma((9,)), dma((4,)), dma((4,)), dma((4,)), dma((4,)),
         dma((5,)), dma((5, RING - 1)), dma((2,)), dma((2, RING)), dma((3,)), dma((3,)),
         dma((5,)), dma((5, RING - 1)), dma((2,)), dma((2, RING)),
         dma((4,)), dma((4,)), dma((4,)), dma((10,)),

time: 136 us -> 136 us (level)
  no operation moved by 1% of the time
where the time goes in v5:
time: 136 us
  Pallas kernels  135 us (99%)
    pallas_call x1, Pallas kernels, shards(): pl.pallas_call(functools.partial(layer_kernel, n_wide, factor), out_shape...  125 us
    pallas_call x1, Pallas kernels, shards(): pl.pallas_call(write_kernel, out_shape=[jax.ShapeDtypeStruct(tokens.shape...  10.1 us

profile of v5, /device:TPU:0, one launch (start us, length us, event | category | flops | bytes accessed | tf_op | source)
XLA Modules:
  0.0 135.5 jit_solution(4928161493544462948)
XLA Ops:
  0.7 124.6 %layer.1 = (bf16[2,64,768]{2,1,0:T(8,128)(2,1)S(1)}, bf16[2,64,768]{2,1,0:T(8,128)(2,1)S(1)}, bf16[2,8,192,768]{3,2,1,0:T(8,128)(2,1)S(1)}, bf16[2,8,96,1536]{3,...) custom-call(bf16[2,64,768]{2,1,0:T(8,128)(2,1)} %refs_0_.1, ...), custom_call_target="tpu_custom_call" | custom-call | tf_op jit(solution)/shard_map/layer/pallas_call | solution.py:783
  125.3 10.1 %write.1 = (bf16[2,64,768]{2,1,0:T(8,128)(2,1)}, bf16[2,64,768]{2,1,0:T(8,128)(2,1)}, f32[768]{0:T(1024)}, f32[768]{0:T(1024)}, f32[768,2304]{1,0:T(8,128)}, /*i...) custom-call(bf16[2,64,768]{2,1,0:T(8,128)(2,1)S(1)} %get-tuple-eleme, ...), custom_call_target="tpu_custom_call" | custom-call | tf_op jit(solution)/shard_map/write/pallas_call | solution.py:798

commit v6 on v5

--- a/solution.py
+++ b/solution.py
@@ -116,7 +116,7 @@
         pltpu.make_async_copy(fb1_h.at[pl.ds(i * width, width)], vecs.at[8 + i], v_sem.at[8 + i]) for i in range(2 * ffh // width)
     ]
     g1, b1, qb, vb, ob, g2, b2, fb2 = (vecs.at[pl.ds(i, 1), :] for i in range(8))
-    for load in small_loads + loads:
+    for load in small_loads + loads[:3]:
         load.start()
 
     def remote(src, dst, send, recv, dev):
@@ -138,6 +138,8 @@
     first = [[entry(0, k, y, core) for k in range(3)], [entry(1, k, 1 - y, ydev) for k in range(3)], [onward(k) for k in range(3)]]
     for trio in first[:2]:
         trio[1].start()
+    for load in loads[3:]:
+        load.start()
     for load in marks:
         load.wait()
     lane64 = lax.broadcasted_iota(jnp.int32, (1, slots), 1)

time: 136 us -> 136 us (level)
  no operation moved by 1% of the time
where the time goes in v6:
time: 136 us
  Pallas kernels  135 us (99%)
    pallas_call x1, Pallas kernels, shards(): pl.pallas_call(functools.partial(layer_kernel, n_wide, factor), out_shape...  125 us
    pallas_call x1, Pallas kernels, shards(): pl.pallas_call(write_kernel, out_shape=[jax.ShapeDtypeStruct(tokens.shape...  10.1 us

profile of v6, /device:TPU:0, one launch (start us, length us, event | category | flops | bytes accessed | tf_op | source)
XLA Modules:
  0.0 135.5 jit_solution(15931964878458166024)
XLA Ops:
  0.7 124.6 %layer.1 = (bf16[2,64,768]{2,1,0:T(8,128)(2,1)S(1)}, bf16[2,64,768]{2,1,0:T(8,128)(2,1)S(1)}, bf16[2,8,192,768]{3,2,1,0:T(8,128)(2,1)S(1)}, bf16[2,8,96,1536]{3,...) custom-call(bf16[2,64,768]{2,1,0:T(8,128)(2,1)} %refs_0_.1, ...), custom_call_target="tpu_custom_call" | custom-call | tf_op jit(solution)/shard_map/layer/pallas_call | solution.py:785
  125.3 10.1 %write.1 = (bf16[2,64,768]{2,1,0:T(8,128)(2,1)}, bf16[2,64,768]{2,1,0:T(8,128)(2,1)}, f32[768]{0:T(1024)}, f32[768]{0:T(1024)}, f32[768,2304]{1,0:T(8,128)}, /*i...) custom-call(bf16[2,64,768]{2,1,0:T(8,128)(2,1)S(1)} %get-tuple-eleme, ...), custom_call_target="tpu_custom_call" | custom-call | tf_op jit(solution)/shard_map/write/pallas_call | solution.py:800
